TPU v7x, 32 devices: a whole 2x2x4 slice. The times are simulated.
32 devices in a mesh: tm: 4 (over y, x), atom: 8 (over z, core).
Axes of the slice: x: 2, y: 2, z: 4, core: 2. Of those that a mesh axis runs over, the one named last changes fastest.
Arguments:
- positions: float32 [256, 3, 12288], P('tm', None, 'atom'), may hold values from -0.5 to 1.5, as said below
- species: int32 [12288], P('atom'), may hold values from 0 to 1
- lengths: float32 [2], replicated, may hold values from 0.5 to 2
- wave_numbers: int32 [3, 16], replicated, may hold values from 1 to 16
- lag_list: int32 [128], replicated, may hold values from 0 to 64, as said below
Outputs:
- structure_function: float32 [4096, 128], P('atom')
Inputs may be any that keep to these rules, and one draw needn't show every extreme that they name: `positions`: every coordinate lies within the stated bounds. `lag_list`: the first entry is 64; lags may repeat.
All inputs are finite; a program needn't handle non-finite values.
Results may differ from a plain program's by a relative error of at most 0.00043.
Values sent between devices are 32-bit elements; how exact they have to be, the bound alone decides.
No kernel may reach another device: no remote copies, remote signals or barrier semaphores. Data moves between devices by JAX's collectives and lax.ppermute only.
A program may use at most 64 MiB of HBM per device.

v0:
```python
import math

import jax
import jax.numpy as jnp
from jax import lax
from jax.sharding import PartitionSpec as P

TWO_PI = 2.0 * math.pi


def shifted(block, axis, distance):
    devices = range(lax.axis_size(axis))
    route = [(i - distance, i) for i in devices if i - distance in devices]
    return lax.ppermute(block, axis, route)


def atom_weight(species, lengths):
    labels = jnp.arange(lengths.shape[0], dtype=jnp.int32)
    return jnp.sum(jnp.where(species[None, :] == labels[:, None], lengths[:, None], 0.0), axis=0)


def density_rows(positions, weight, wave_numbers, count):
    width = wave_numbers.shape[1]
    pairs = count // width
    frames, _, atoms = positions.shape
    scaled = TWO_PI * wave_numbers.astype(jnp.float32)
    groups = positions.reshape(frames // 4, 4, 3, atoms)

    def one_group(block):
        angle = scaled[None, :, :, None] * block[:, :, None, :]
        cosine = jnp.cos(angle)
        sine = jnp.sin(angle)
        cos_x = jnp.repeat(cosine[:, 0], width, axis=1)
        sin_x = jnp.repeat(sine[:, 0], width, axis=1)
        cos_y = jnp.tile(cosine[:, 1], (1, width, 1))
        sin_y = jnp.tile(sine[:, 1], (1, width, 1))
        real = cos_x * cos_y - sin_x * sin_y
        imag = cos_x * sin_y + sin_x * cos_y
        left = jnp.concatenate([real, imag], axis=1).astype(jnp.bfloat16)
        right = jnp.concatenate(
            [weight[None, None, :] * cosine[:, 2], weight[None, None, :] * sine[:, 2]], axis=1
        ).astype(jnp.bfloat16)
        prod = jnp.einsum("gpa,gna->gpn", left, right, preferred_element_type=jnp.float32)
        rho_re = prod[:, :pairs, :width] - prod[:, pairs:, width:]
        rho_im = prod[:, :pairs, width:] + prod[:, pairs:, :width]
        return (rho_re.reshape(4, count), rho_im.reshape(4, count))

    rho_re, rho_im = lax.map(one_group, groups)
    return jnp.concatenate([rho_re.reshape(frames, count), rho_im.reshape(frames, count)], axis=0).T


def on_device(positions, species, lengths, wave_numbers, lag_list):
    weight = atom_weight(species, lengths)
    frames = positions.shape[0]
    width = wave_numbers.shape[1]
    total_q = width**3
    share = total_q // lax.axis_size("atom")
    summed = lax.psum(density_rows(positions, weight, wave_numbers, total_q), "atom")
    own = lax.dynamic_slice_in_dim(summed, lax.axis_index("atom") * share, share, 0)
    reach = lax.axis_size("tm") // 4
    blocks = [own]
    for step in range(1, reach + 1):
        blocks.append(shifted(own, "tm", -step))
    own_re = own[:, :frames]
    own_im = own[:, frames:]
    frame_ids = jnp.arange(frames, dtype=jnp.int32)
    summed_lags = jnp.zeros((share, lag_list.shape[0]), jnp.float32)
    for offset_block, partner in enumerate(blocks):
        product = (
            own_re[:, :, None] * partner[:, None, :frames]
            + own_im[:, :, None] * partner[:, None, frames:]
        )
        offsets = offset_block * frames + frame_ids[None, :] - frame_ids[:, None]
        select = (
            (offsets[:, :, None] == lag_list[None, None, :])
            .astype(jnp.float32)
            .reshape(frames * frames, -1)
        )
        summed_lags = summed_lags + jnp.dot(
            product.reshape(share, frames * frames),
            select,
            precision=lax.Precision.HIGHEST,
            preferred_element_type=jnp.float32,
        )
    whole_frames = frames * lax.axis_size("tm")
    atoms_all = positions.shape[2] * lax.axis_size("atom")
    denominator = (whole_frames - lag_list).astype(jnp.float32) * atoms_all
    return lax.psum(summed_lags / denominator[None, :], "tm")


def solution(mesh):
    placed = (P("tm", None, "atom"), P("atom"), P(), P(), P())
    return jax.shard_map(
        on_device, mesh=mesh, in_specs=placed, out_specs=P("atom", None), check_vma=False
    )
```

profile of v0, /device:TPU:0, one launch (start us, length us, event | category | flops | bytes accessed | tf_op | source)
XLA Modules:
  0.0 320.5 jit_solution(5219921571370523185)
XLA Ops:
  9.7 168.2 %while.12 = (s32[]{:T(128)}, f32[16,4,4096]{2,1,0:T(4,128)}, f32[16,4,4096]{2,1,0:T(4,128)S(1)}, f32[3,16]{1,0:T(4,128)S(1)}, f32[16,4,3,1536]{3,1,0,2:T(4,128)S(1)}, /*index=5*/f32[1536]{0:T(1024)S(1)}, s32[]{:T(128)}) while((s32[]{:T(128)}, f32[16,4,4096]{2,1,0:T(4,128)}, f32[16,4,4096]{2,1,0:T(4,128)S(1)}, f32[3,16]{1,0:T(4,128)S(1)}, ...), condition=%wide.region_2.3_spmd, body=%wide.region_1.2_spmd.sunk | while | flops 227999744 | bytes 22903068 | solution.py:48
  9.7 4.1 %multiply_cosine_fusion.2 = (f32[4,3,16,1536]{3,2,0,1:T(8,128)S(1)}, f32[4,3,16,1536]{3,2,0,1:T(8,128)S(1)}) fusion(f32[4,3,1536]{2,0,1:T(4,128)S(1)} %dynamic-slice_bitcast_fusion.2, f32[3,16]{1,0:T(4,128)S(1)} %get-tuple-element.164), kind=kLoop, calls=%fused_computation.7.clone.1 | loop fusion | flops 294912 | bytes 2433216 | tf_op jit(solution)/shard_map/while/body/eval_jaxpr/cos | solution.py:31
  16.3 2.3 fusion.63
  20.2 4.1 %multiply_cosine_fusion.2 = (f32[4,3,16,1536]{3,2,0,1:T(8,128)S(1)}, f32[4,3,16,1536]{3,2,0,1:T(8,128)S(1)}) fusion(f32[4,3,1536]{2,0,1:T(4,128)S(1)} %dynamic-slice_bitcast_fusion.2, f32[3,16]{1,0:T(4,128)S(1)} %get-tuple-element.164), kind=kLoop, calls=%fused_computation.7.clone.1 | loop fusion | flops 294912 | bytes 2433216 | tf_op jit(solution)/shard_map/while/body/eval_jaxpr/cos | solution.py:31
  26.8 2.3 fusion.63
  30.7 4.1 %multiply_cosine_fusion.2 = (f32[4,3,16,1536]{3,2,0,1:T(8,128)S(1)}, f32[4,3,16,1536]{3,2,0,1:T(8,128)S(1)}) fusion(f32[4,3,1536]{2,0,1:T(4,128)S(1)} %dynamic-slice_bitcast_fusion.2, f32[3,16]{1,0:T(4,128)S(1)} %get-tuple-element.164), kind=kLoop, calls=%fused_computation.7.clone.1 | loop fusion | flops 294912 | bytes 2433216 | tf_op jit(solution)/shard_map/while/body/eval_jaxpr/cos | solution.py:31
  41.3 4.1 %multiply_cosine_fusion.2 = (f32[4,3,16,1536]{3,2,0,1:T(8,128)S(1)}, f32[4,3,16,1536]{3,2,0,1:T(8,128)S(1)}) fusion(f32[4,3,1536]{2,0,1:T(4,128)S(1)} %dynamic-slice_bitcast_fusion.2, f32[3,16]{1,0:T(4,128)S(1)} %get-tuple-element.164), kind=kLoop, calls=%fused_computation.7.clone.1 | loop fusion | flops 294912 | bytes 2433216 | tf_op jit(solution)/shard_map/while/body/eval_jaxpr/cos | solution.py:31
  51.8 4.1 %multiply_cosine_fusion.2 = (f32[4,3,16,1536]{3,2,0,1:T(8,128)S(1)}, f32[4,3,16,1536]{3,2,0,1:T(8,128)S(1)}) fusion(f32[4,3,1536]{2,0,1:T(4,128)S(1)} %dynamic-slice_bitcast_fusion.2, f32[3,16]{1,0:T(4,128)S(1)} %get-tuple-element.164), kind=kLoop, calls=%fused_computation.7.clone.1 | loop fusion | flops 294912 | bytes 2433216 | tf_op jit(solution)/shard_map/while/body/eval_jaxpr/cos | solution.py:31
  62.3 4.1 %multiply_cosine_fusion.2 = (f32[4,3,16,1536]{3,2,0,1:T(8,128)S(1)}, f32[4,3,16,1536]{3,2,0,1:T(8,128)S(1)}) fusion(f32[4,3,1536]{2,0,1:T(4,128)S(1)} %dynamic-slice_bitcast_fusion.2, f32[3,16]{1,0:T(4,128)S(1)} %get-tuple-element.164), kind=kLoop, calls=%fused_computation.7.clone.1 | loop fusion | flops 294912 | bytes 2433216 | tf_op jit(solution)/shard_map/while/body/eval_jaxpr/cos | solution.py:31
  68.8 2.3 fusion.63
  72.8 4.1 %multiply_cosine_fusion.2 = (f32[4,3,16,1536]{3,2,0,1:T(8,128)S(1)}, f32[4,3,16,1536]{3,2,0,1:T(8,128)S(1)}) fusion(f32[4,3,1536]{2,0,1:T(4,128)S(1)} %dynamic-slice_bitcast_fusion.2, f32[3,16]{1,0:T(4,128)S(1)} %get-tuple-element.164), kind=kLoop, calls=%fused_computation.7.clone.1 | loop fusion | flops 294912 | bytes 2433216 | tf_op jit(solution)/shard_map/while/body/eval_jaxpr/cos | solution.py:31
  83.3 4.1 %multiply_cosine_fusion.2 = (f32[4,3,16,1536]{3,2,0,1:T(8,128)S(1)}, f32[4,3,16,1536]{3,2,0,1:T(8,128)S(1)}) fusion(f32[4,3,1536]{2,0,1:T(4,128)S(1)} %dynamic-slice_bitcast_fusion.2, f32[3,16]{1,0:T(4,128)S(1)} %get-tuple-element.164), kind=kLoop, calls=%fused_computation.7.clone.1 | loop fusion | flops 294912 | bytes 2433216 | tf_op jit(solution)/shard_map/while/body/eval_jaxpr/cos | solution.py:31
  93.8 4.1 %multiply_cosine_fusion.2 = (f32[4,3,16,1536]{3,2,0,1:T(8,128)S(1)}, f32[4,3,16,1536]{3,2,0,1:T(8,128)S(1)}) fusion(f32[4,3,1536]{2,0,1:T(4,128)S(1)} %dynamic-slice_bitcast_fusion.2, f32[3,16]{1,0:T(4,128)S(1)} %get-tuple-element.164), kind=kLoop, calls=%fused_computation.7.clone.1 | loop fusion | flops 294912 | bytes 2433216 | tf_op jit(solution)/shard_map/while/body/eval_jaxpr/cos | solution.py:31
  104.3 4.1 %multiply_cosine_fusion.2 = (f32[4,3,16,1536]{3,2,0,1:T(8,128)S(1)}, f32[4,3,16,1536]{3,2,0,1:T(8,128)S(1)}) fusion(f32[4,3,1536]{2,0,1:T(4,128)S(1)} %dynamic-slice_bitcast_fusion.2, f32[3,16]{1,0:T(4,128)S(1)} %get-tuple-element.164), kind=kLoop, calls=%fused_computation.7.clone.1 | loop fusion | flops 294912 | bytes 2433216 | tf_op jit(solution)/shard_map/while/body/eval_jaxpr/cos | solution.py:31
  114.8 4.1 %multiply_cosine_fusion.2 = (f32[4,3,16,1536]{3,2,0,1:T(8,128)S(1)}, f32[4,3,16,1536]{3,2,0,1:T(8,128)S(1)}) fusion(f32[4,3,1536]{2,0,1:T(4,128)S(1)} %dynamic-slice_bitcast_fusion.2, f32[3,16]{1,0:T(4,128)S(1)} %get-tuple-element.164), kind=kLoop, calls=%fused_computation.7.clone.1 | loop fusion | flops 294912 | bytes 2433216 | tf_op jit(solution)/shard_map/while/body/eval_jaxpr/cos | solution.py:31
  125.3 4.1 %multiply_cosine_fusion.2 = (f32[4,3,16,1536]{3,2,0,1:T(8,128)S(1)}, f32[4,3,16,1536]{3,2,0,1:T(8,128)S(1)}) fusion(f32[4,3,1536]{2,0,1:T(4,128)S(1)} %dynamic-slice_bitcast_fusion.2, f32[3,16]{1,0:T(4,128)S(1)} %get-tuple-element.164), kind=kLoop, calls=%fused_computation.7.clone.1 | loop fusion | flops 294912 | bytes 2433216 | tf_op jit(solution)/shard_map/while/body/eval_jaxpr/cos | solution.py:31
  135.8 4.1 %multiply_cosine_fusion.2 = (f32[4,3,16,1536]{3,2,0,1:T(8,128)S(1)}, f32[4,3,16,1536]{3,2,0,1:T(8,128)S(1)}) fusion(f32[4,3,1536]{2,0,1:T(4,128)S(1)} %dynamic-slice_bitcast_fusion.2, f32[3,16]{1,0:T(4,128)S(1)} %get-tuple-element.164), kind=kLoop, calls=%fused_computation.7.clone.1 | loop fusion | flops 294912 | bytes 2433216 | tf_op jit(solution)/shard_map/while/body/eval_jaxpr/cos | solution.py:31
  146.3 4.1 %multiply_cosine_fusion.2 = (f32[4,3,16,1536]{3,2,0,1:T(8,128)S(1)}, f32[4,3,16,1536]{3,2,0,1:T(8,128)S(1)}) fusion(f32[4,3,1536]{2,0,1:T(4,128)S(1)} %dynamic-slice_bitcast_fusion.2, f32[3,16]{1,0:T(4,128)S(1)} %get-tuple-element.164), kind=kLoop, calls=%fused_computation.7.clone.1 | loop fusion | flops 294912 | bytes 2433216 | tf_op jit(solution)/shard_map/while/body/eval_jaxpr/cos | solution.py:31
  156.8 4.1 %multiply_cosine_fusion.2 = (f32[4,3,16,1536]{3,2,0,1:T(8,128)S(1)}, f32[4,3,16,1536]{3,2,0,1:T(8,128)S(1)}) fusion(f32[4,3,1536]{2,0,1:T(4,128)S(1)} %dynamic-slice_bitcast_fusion.2, f32[3,16]{1,0:T(4,128)S(1)} %get-tuple-element.164), kind=kLoop, calls=%fused_computation.7.clone.1 | loop fusion | flops 294912 | bytes 2433216 | tf_op jit(solution)/shard_map/while/body/eval_jaxpr/cos | solution.py:31
  167.3 4.1 %multiply_cosine_fusion.2 = (f32[4,3,16,1536]{3,2,0,1:T(8,128)S(1)}, f32[4,3,16,1536]{3,2,0,1:T(8,128)S(1)}) fusion(f32[4,3,1536]{2,0,1:T(4,128)S(1)} %dynamic-slice_bitcast_fusion.2, f32[3,16]{1,0:T(4,128)S(1)} %get-tuple-element.164), kind=kLoop, calls=%fused_computation.7.clone.1 | loop fusion | flops 294912 | bytes 2433216 | tf_op jit(solution)/shard_map/while/body/eval_jaxpr/cos | solution.py:31
  181.4 67.6 %all-reduce.3.cloned.1.call-done = f32[4096,128]{0,1:T(8,128)} async-done(((f32[4096,128]{0,1:T(8,128)}), f32[4096,128]{0,1:T(8,128)}) %all-reduce.3.cloned.1.call-update) | async-done | bytes 2097168 | tf_op jit(solution)/shard_map/psum | solution.py:58
  252.5 7.3 %fusion.30 = f32[512,128]{1,0:T(8,128)S(1)} fusion(f32[512,64]{0,1:T(8,128)S(1)} %get-tuple-element.79, f32[512,64]{0,1:T(8,128)S(1)} %get-tuple-element.78, s32[128]{0:T(128)S(1)} %copy-done, s32[64,64]{1,0:T(8,128)S(1)} %iota_subtract_fusion.1), kind=kOutput, calls=%fused_computation.46 | convolution fusion | flops 3228041216 | bytes 541184 | tf_op jit(solution)/shard_map/dot_general | solution.py:79
  259.8 8.2 %fusion.45 = f32[512,128]{1,0:T(8,128)} fusion(f32[512,128]{1,0:T(8,128)S(1)} %fusion.30, f32[512,64]{0,1:T(8,128)S(1)} %get-tuple-element.81, f32[512,64]{0,1:T(8,128)S(1)} %get-tuple-element.80, f32[512,64]{0,1:T(8,128)S(1)} %get-tuple-element.79, f32[512,64]{0,1:T(8,128)S(1)} %get-tuple-element.78, s32[64,64]{1,0:T(8,128)S(1)} %iota_subtract_fusion, ...), kind=kOutput, calls=%fused_computation.49 | convolution fusion | flops 3228172288 | bytes 1065984 | tf_op jit(solution)/shard_map/dot_general | solution.py:79
  268.1 43.9 %all-reduce.5.cloned.1.call-done = f32[512,128]{1,0:T(8,128)} async-done(((f32[512,128]{1,0:T(8,128)}), f32[512,128]{1,0:T(8,128)}) %all-reduce.5.cloned.1.call-update) | async-done | bytes 262160 | tf_op jit(solution)/shard_map/psum | solution.py:88
  (213 shorter events, 105.9 us)
Async XLA Ops:
  6.5 242.5 %all-reduce.3.cloned.1.call-start = ((), (), s32[]{:S(2)}) async-start(), calls=%async_computation | async-start | bytes 4194304 | tf_op jit(solution)/shard_map/psum | solution.py:58
  179.8 1.6 copy-start
  181.3 130.7 %all-reduce.5.cloned.1.call-start = ((), (), s32[]{:S(2)}) async-start(), calls=%async_computation.1 | async-start | bytes 524288 | tf_op jit(solution)/shard_map/psum | solution.py:88
  250.0 9.8 %collective-permute-start = (f32[512,128]{0,1:T(8,128)S(1)}, f32[512,128]{0,1:T(8,128)S(1)}, u32[]{:S(2)}, u32[]{:S(2)}) collective-permute-start(f32[512,128]{0,1:T(8,128)S(1)} %constant_dynamic-slice_fusion.1), channel_id=1, source_target_pairs={{8,0},{16,8},{24,16},{9,1},{17,9},{25,17},{10,2},{18,10},{26,18},{... | collective-permute-start | bytes 786440 | tf_op jit(solution)/shard_map/ppermute | solution.py:14
Sparse Core Ops, SparseCore 0:
  181.4 67.5 all-reduce.2
  268.2 43.7 all-reduce.4
where the time goes:
time: 321 us
  waiting for transfers between devices  112 us (35%)
  other arithmetic  106 us (33%)
  matrix products  51.9 us (16%)
  local copies, waits for them, and re-layouts  35.4 us (11%)
  between operations  13.5 us (4%)
    psum x1, waiting for transfers between devices, on_device(): lax.psum(density_rows(positions, weight, wave_numbers, total_q), 'atom')  67.6 us
    cos x16, other arithmetic, one_group(): cosine = jnp.cos(angle)  66.2 us
    psum x1, waiting for transfers between devices, on_device(): return lax.psum(summed_lags / denominator[None, :], 'tm')  43.9 us
    dot_general x16, matrix products, one_group(): jnp.einsum('gpa,gna->gpn', left, right, preferred_element_type=jnp.float32)  36.3 us
    another operation x34, other arithmetic  36 us
    dot_general x2, matrix products, on_device(): jnp.dot(product.reshape(share, frames * frames), select, precision=lax.Pr...  15.5 us
    dynamic_update_slice x16, local copies, waits for them, and re-layouts, density_rows(): rho_re, rho_im = lax.map(one_group, groups)  10.2 us
    broadcast_in_dim x32, local copies, waits for them, and re-layouts, density_rows(): rho_re, rho_im = lax.map(one_group, groups)  9.5 us
  transfers between devices with their start and end apart: 3, of which 2 were waited for; matrix products, arithmetic and copies ran while one was open for 3% of the time, Pallas kernels for 0%

commit v1 on v0

v1 whole, which is shorter than its diff:
```python
import functools
import math

import jax
import jax.numpy as jnp
import numpy as np
from jax import lax
from jax.experimental import pallas as pl
from jax.experimental.pallas import tpu as pltpu
from jax.sharding import PartitionSpec as P

COS = (1.0, -19.73920440673828, 64.93911743164062, -85.45014190673828, 60.16762924194336, -25.967599868774414, 6.528658390045166)
SIN = (6.2831854820251465, -41.34170150756836, 81.60513305664062, -76.70301818847656, 42.02592849731445, -14.899847030639648, 3.2381374835968018)

CHUNKS = 2
PITCH = 17
WIDE = 33
VMEM_LIMIT = 48 << 20


def polynomial(coefficients, s):
    value = coefficients[-1] * s + coefficients[-2]
    for c in coefficients[-3::-1]:
        value = value * s + c
    return value


def circle(turns):
    r = turns - jnp.round(turns)
    s = r * r
    return polynomial(COS, s), polynomial(SIN, s) * r


def tables(x, y, z, weight, put_x, put_y, put_z):
    c, s = circle(0.5 * x)
    twice = 4.0 * c * c - 2.0
    cs = [c, (twice - 1.0) * c]
    ss = [s, (twice + 1.0) * s]
    for _ in range(6):
        cs.append(twice * cs[-1] - cs[-2])
        ss.append(twice * ss[-1] - ss[-2])
    for m in range(8):
        put_x(m, cs[m])
        put_x(8 + m, ss[m])
    c, s = circle(0.5 * y)
    twice = 4.0 * c * c - 2.0
    for l, value in enumerate((c, s, (twice - 1.0) * c, (twice + 1.0) * s)):
        put_y(l, value)
    c2 = 0.5 * twice * twice - 1.0
    s2 = 2.0 * twice * s * c
    four = 4.0 * c2 * c2
    for h, value in enumerate((c2, s2, c2 * (four - 3.0), s2 * (four - 1.0))):
        put_y(4 + h, value)
    real, imag = circle(8.5 * (x + y))
    c, s = circle(z)
    twice = c + c
    cs = [c, twice * c - 1.0]
    ss = [s, twice * s]
    for _ in range(14):
        cs.append(twice * cs[-1] - cs[-2])
        ss.append(twice * ss[-1] - ss[-2])
    for k in range(16):
        c = (weight * cs[k]).astype(jnp.bfloat16).astype(jnp.float32)
        s = (weight * ss[k]).astype(jnp.bfloat16).astype(jnp.float32)
        put_z(k, real * c - imag * s)
        put_z(16 + k, real * s + imag * c)


def split(value):
    high = value.astype(jnp.bfloat16)
    return high, (value - high.astype(jnp.float32)).astype(jnp.bfloat16)


def slot_of(k):
    return jnp.where(k >= 9, k - 9, 16 - k)


def turned(value, quarter):
    return pltpu.roll(value, 64, 1) * quarter


def density_kernel(me_ref, wave_ref, own_ref, sibling_ref, keep_ref, send_ref, xs, ys, zs, prod, grid, *, first, bits, shift):
    sources = (own_ref, sibling_ref)
    rows = (own_ref.shape[0] - 8) // 3
    tiles = own_ref.shape[1] // 128
    base = pl.multiple_of((first + pl.program_id(0)) * 8, 8)
    for i, source in enumerate(sources):

        def one_tile(j, carry):
            lanes = pl.ds(pl.multiple_of(j * 128, 128), 128)
            x = source[pl.ds(base, 8), lanes]
            y = source[pl.ds(base + rows, 8), lanes]
            z = source[pl.ds(base + 2 * rows, 8), lanes]
            weight = source[pl.ds(3 * rows, 8), lanes]

            def put(ref, pitch):
                def go(f, value):
                    ref[i * tiles + j, pl.ds(f, 8, stride=pitch), :] = value

                return go

            tables(x, y, z, weight, put(xs, PITCH), put(ys, PITCH), put(zs, WIDE))
            return carry

        lax.fori_loop(0, tiles, one_tile, 0, unroll=2)

    def one_frame(f, carry):
        r0 = f * PITCH
        total = jnp.zeros((128, 128), jnp.float32)
        for pair in range(len(sources) * tiles // 2):
            left, right = [], []
            for t in (2 * pair, 2 * pair + 1):
                x = xs[t, pl.ds(r0, 16), :]
                z = zs[t, pl.ds(f * WIDE, 32), :]
                exact = jnp.concatenate([x * ys[t, pl.ds(r0 + l, 1), :] for l in range(4)], 0)
                left.append(jnp.concatenate(split(exact), 0))
                hs = [ys[t, pl.ds(r0 + 4 + h, 1), :] for h in range(4)]
                right.append(jnp.concatenate([part * h for part in (z[:16], z[16:]) for h in hs], 0).astype(jnp.bfloat16))
            total = total + lax.dot_general(
                jnp.concatenate(left, 1),
                jnp.concatenate(right, 1),
                (((1,), (1,)), ((), ())),
                preferred_element_type=jnp.float32,
            )
        prod[f] = total[:64] + total[64:]
        return carry

    lax.fori_loop(0, 8, one_frame, 0, unroll=8)

    lane = lax.broadcasted_iota(jnp.int32, (8, 128), 1)
    quarter = jnp.where(lane < 64, -1.0, 1.0).astype(jnp.float32)
    for f in range(8):
        for l in range(4):
            cosine = prod[f, l * 16 : l * 16 + 8, :]
            sine = turned(prod[f, l * 16 + 8 : l * 16 + 16, :], quarter)
            r = (f * 4 + l) * PITCH
            grid[r : r + 8, :] = cosine + sine
            grid[r + 8 : r + 16, :] = cosine - sine

    me = me_ref[0]
    for i in range(8):
        flip = sum(((i >> (2 - j)) & 1) << bit for j, bit in enumerate(bits))
        pair = (me ^ flip) >> shift
        out_ref = keep_ref if i < 4 else send_ref
        for j in range(2):
            slot = slot_of(wave_ref[0, 2 * pair + j])
            for f in range(8):
                out_ref[f, i % 4, 4 * j : 4 * j + 4, :] = grid[pl.ds(f * 4 * PITCH + slot, 4, stride=PITCH), :]


def density(me, wave_numbers, own, sibling, first, groups, bits, shift):
    tiles = 2 * own.shape[1] // 128
    table = pltpu.VMEM((tiles, 8 * PITCH, 128), jnp.float32)
    block = pl.BlockSpec((8, 4, 8, 128), lambda g: (g, 0, 0, 0))
    shape = jax.ShapeDtypeStruct((groups * 8, 4, 8, 128), jnp.float32)
    frames = groups * 8
    return pl.pallas_call(
        functools.partial(density_kernel, first=first, bits=bits, shift=shift),
        grid=(groups,),
        out_shape=(shape, shape),
        in_specs=[pl.BlockSpec(memory_space=pltpu.SMEM)] * 2 + [pl.BlockSpec(own.shape, lambda g: (0, 0))] * 2,
        out_specs=(block, block),
        scratch_shapes=[
            table,
            table,
            pltpu.VMEM((tiles, 8 * WIDE, 128), jnp.float32),
            pltpu.VMEM((8, 64, 128), jnp.float32),
            pltpu.VMEM((32 * PITCH, 128), jnp.float32),
        ],
        compiler_params=pltpu.CompilerParams(vmem_limit_bytes=VMEM_LIMIT),
        cost_estimate=pl.CostEstimate(flops=frames * tiles * 128 * 64 * 128 * 2 * 8, bytes_accessed=frames * 32768, transcendentals=0),
        name="density",
    )(me, wave_numbers, own, sibling)


def combine(value, swap, second, quarter):
    mixed = jnp.where(second, turned(value, quarter), value)
    return swap(mixed) + jnp.where(second, -mixed, mixed)


def waves_kernel(*refs, terms):
    parts, outs = refs[:terms], refs[terms:]
    frames = parts[0].shape[0]
    row = lax.broadcasted_iota(jnp.int32, (8, 128), 0)
    lane = lax.broadcasted_iota(jnp.int32, (8, 128), 1)
    quarter = jnp.where(lane < 64, -1.0, 1.0).astype(jnp.float32)
    bit_l, bit_h = (row & 1) == 1, (lane & 16) == 16

    def swap(axis, distance, second):
        size = (8, 128)[axis]

        def go(value):
            return jnp.where(second, pltpu.roll(value, distance, axis), pltpu.roll(value, size - distance, axis))

        return go

    for g, out in enumerate(outs):
        for t in range(frames):
            value = parts[0][t, g]
            for part in parts[1:]:
                value = value + part[t, g]
            value = combine(value, swap(0, 1, bit_l), bit_l, quarter)
            value = combine(value, swap(1, 16, bit_h), bit_h, quarter)
            out[:, t, :] = value


def waves(parts, groups):
    frames = parts[0].shape[0]
    shape = jax.ShapeDtypeStruct((8, frames, 128), jnp.float32)
    return pl.pallas_call(
        functools.partial(waves_kernel, terms=len(parts)),
        grid=(1,),
        out_shape=(shape,) * groups,
        in_specs=[pl.BlockSpec((frames, groups, 8, 128), lambda g: (0, 0, 0, 0))] * len(parts),
        out_specs=(pl.BlockSpec((8, frames, 128), lambda g: (0, 0, 0)),) * groups,
        compiler_params=pltpu.CompilerParams(vmem_limit_bytes=VMEM_LIMIT),
        name="waves",
    )(*parts)


def lags_kernel(place_ref, wave_ref, lag_ref, basis_ref, *refs, blocks, frames, atoms, period, share):
    parts, (out_ref, series, result) = refs[:blocks], refs[blocks:]
    half = period // 2
    tm, me = place_ref[0], place_ref[1]
    chunk = parts[0].shape[2]
    steps = blocks // CHUNKS
    per_block = frames // steps
    for p in range(steps):
        for c in range(CHUNKS):
            for side in range(2):
                core = (me & 1) ^ side
                start = (tm ^ p) * per_block + core * (per_block // 2) + c * chunk
                series[:, pl.ds(pl.multiple_of(start, chunk), chunk), :] = parts[p * CHUNKS + c][side]
    lane = lax.broadcasted_iota(jnp.int32, (8, 128), 1)
    source = lane
    for n in range(16):
        source = jnp.where((lane & 15) == n, lane - n + wave_ref[2, n] - 1, source)
    order = 2 * lax.broadcasted_iota(jnp.int32, (half, 128), 0) + 1
    lag = lag_ref[...]
    phase = (order * lag).astype(jnp.float32)
    turns = phase - jnp.round(phase * (0.5 / period)) * (2.0 * period)
    cosine, _ = circle(turns * (0.5 / period))
    scale = (2.0 / period) / ((frames - lag).astype(jnp.float32) * float(atoms))
    cosine = cosine * scale
    for l in range(4):
        powers = []
        for a in range(2):
            high, low = split(series[4 * a + l])
            spectrum = jnp.dot(basis_ref[...], jnp.concatenate([high, high, low], 0), preferred_element_type=jnp.float32)
            power = spectrum[:half] * spectrum[:half] + spectrum[half:] * spectrum[half:]
            powers.append(power + pltpu.roll(power, 64, 1))
        power = jnp.concatenate(
            [
                jnp.take_along_axis(jnp.where(lane < 64, powers[0][i : i + 8], powers[1][i : i + 8]), source, axis=1)
                for i in range(0, half, 8)
            ],
            0,
        )
        result[l] = jnp.dot(power.T, cosine, precision=lax.Precision.HIGHEST, preferred_element_type=jnp.float32)
    for i in range(share // 16):
        block = (me * (share // 16) + i) % 32
        k = wave_ref[1, block % 16] - 1
        hi, lo = k // 4, k % 4
        slot = [jnp.where(v == 0, 3, jnp.where(v == 1, 1, jnp.where(v == 2, 0, 2))) for v in (hi, lo)]
        start = pl.multiple_of((block // 16) * 64 + slot[0] * 16, 16)
        out_ref[i * 16 : i * 16 + 16, :] = result[slot[1], pl.ds(start, 16), :]


def lags(place, wave_numbers, lag_list, parts, frames, atoms, period, share):
    half = period // 2
    angle = np.outer(2 * np.arange(half) + 1, np.arange(frames)) * (math.pi / period)
    basis = np.concatenate([np.cos(angle), np.sin(angle)], 0).astype(np.float32)
    high = basis.astype(jnp.bfloat16)
    low = (basis - high.astype(np.float32)).astype(jnp.bfloat16)
    basis = jnp.asarray(np.concatenate([high, low, high], 1))
    smem = pl.BlockSpec(memory_space=pltpu.SMEM)
    vmem = pl.BlockSpec(memory_space=pltpu.VMEM)
    return pl.pallas_call(
        functools.partial(lags_kernel, blocks=len(parts), frames=frames, atoms=atoms, period=period, share=share),
        out_shape=jax.ShapeDtypeStruct((share, lag_list.shape[0]), jnp.float32),
        in_specs=[smem, smem] + [vmem] * (2 + len(parts)),
        out_specs=vmem,
        scratch_shapes=[pltpu.VMEM((8, frames, 128), jnp.float32), pltpu.VMEM((4, 128, lag_list.shape[0]), jnp.float32)],
        compiler_params=pltpu.CompilerParams(vmem_limit_bytes=VMEM_LIMIT),
        name="lags",
    )(place, wave_numbers, lag_list[None, :], basis, *parts)


def swapped(block, axis, flip):
    return lax.ppermute(block, axis, [(i, i ^ flip) for i in range(lax.axis_size(axis))])


def on_device(positions, species, lengths, wave_numbers, lag_list):
    frames, _, atoms = positions.shape
    devices, blocks = lax.axis_size("atom"), lax.axis_size("tm")
    me, tm = lax.axis_index("atom"), lax.axis_index("tm")
    share = wave_numbers.shape[1] ** 3 // devices
    period = (frames * blocks * 5) // 4
    half = frames // 2
    shift = devices.bit_length() - 4
    flips = [1 << bit for bit in range(1, devices.bit_length() - 1)]
    bits = ([bit for bit in range(1, devices.bit_length() - 1) if bit >= shift] + [0])[:3]

    labels = jnp.arange(lengths.shape[0], dtype=jnp.int32)
    weight = jnp.sum(jnp.where(species[None, :] == labels[:, None], lengths[:, None], 0.0), axis=0)
    turned = jnp.transpose(positions, (1, 0, 2))

    def payload(core):
        part = lax.dynamic_slice_in_dim(turned, core * half, half, 1).reshape(3 * half, atoms)
        return jnp.concatenate([part, jnp.broadcast_to(weight[None, :], (8, atoms))], 0)

    own = payload(me & 1)
    sibling = swapped(payload(1 - (me & 1)), "atom", 1)
    place = jnp.stack([tm, me]).astype(jnp.int32)

    groups = half // 8 // CHUNKS
    parts = [[None] * CHUNKS for _ in range(blocks)]
    for c in range(CHUNKS):
        keep, send = density(place[1:2], wave_numbers, own, sibling, c * groups, groups, bits, shift)
        terms, fresh, held = [keep], True, 8
        for flip in flips:
            if flip >= (1 << shift):
                held //= 2
                out = send if fresh else sum(t[:, held : 2 * held] for t in terms)
                fresh = False
                terms = terms + [swapped(out, "atom", flip)]
            else:
                keep, send = (a + swapped(a, "atom", flip) for a in (keep, send))
                terms = [keep]
        final = waves(terms, held)
        mine, other = final[0], final[-1]
        both = jnp.stack([mine, swapped(other, "atom", 1)])
        for p in range(blocks):
            parts[p][c] = both if p == 0 else swapped(both, "tm", p)
    parts = [part for row in parts for part in row]
    return lags(place, wave_numbers, lag_list, parts, frames * blocks, atoms * devices, period, share)


def solution(mesh):
    placed = (P("tm", None, "atom"), P("atom"), P(), P(), P())
    return jax.shard_map(
        on_device, mesh=mesh, in_specs=placed, out_specs=P("atom", None), check_vma=False
    )
```

time: 321 us -> 63.1 us (0.20)
  other arithmetic: 106 us -> 1.02 us
  waiting for transfers between devices: 112 us -> 23.1 us
  matrix products: 51.9 us -> 0 us
  local copies, waits for them, and re-layouts: 35.4 us -> 1.36 us
  Pallas kernels: 0 us -> 21.1 us
  starting transfers between devices: 1.52 us -> 16.1 us
  between operations: 13.5 us -> 0.13 us
    psum x2 -> x0, waiting for transfers between devices: 112 us -> none  [the longest x1 67.6 us: on_device(): lax.psum(density_rows(positions, weight, wave_numbers, total_q), 'atom')]
    cos x16 -> x0, other arithmetic: 66.2 us -> none  [one_group(): cosine = jnp.cos(angle)]
    dot_general x18 -> x0, matrix products: 51.9 us -> none  [the longest x16 36.3 us: one_group(): jnp.einsum('gpa,gna->gpn', left, right, preferred_element_type=jnp.float32)]
    another operation x34 -> x3, other arithmetic: 36 us -> 0.1 us  [the longest x1 0.07 us: on_device(): place = jnp.stack([tm, me]).astype(jnp.int32)]
    ppermute x1 -> x13, waiting for transfers between devices: 0.01 us -> 23.1 us  [swapped(): lax.ppermute(block, axis, [(i, i ^ flip) for i in range(lax.axis_size(axi...]
    pallas_call x0 -> x5, Pallas kernels: none -> 21.1 us  [the longest x2 15.3 us: density(): pl.pallas_call(functools.partial(density_kernel, first=first, bits=bits,...]
    ppermute x1 -> x13, starting transfers between devices: 1.47 us -> 16.1 us  [swapped(): lax.ppermute(block, axis, [(i, i ^ flip) for i in range(lax.axis_size(axi...]
    dynamic_update_slice x16 -> x0, local copies, waits for them, and re-layouts: 10.2 us -> none  [density_rows(): rho_re, rho_im = lax.map(one_group, groups)]
  transfers between devices with their start and end apart: 3 -> 13, of which waited for: 2 -> 8; matrix products, arithmetic and copies ran while one was open for 3% -> 0% of each run, Pallas kernels for 0% -> 13%
where the time goes in v1:
time: 63.1 us; the launch traced here: 62.8 us
  waiting for transfers between devices  23.1 us (37%)
  Pallas kernels  21.1 us (33%)
  starting transfers between devices  16.1 us (26%)
  local copies, waits for them, and re-layouts  1.36 us (2%)
  other arithmetic  1.02 us (2%)
    ppermute x13, waiting for transfers between devices, swapped(): lax.ppermute(block, axis, [(i, i ^ flip) for i in range(lax.axis_size(axi...  23.1 us
    ppermute x13, starting transfers between devices, swapped(): lax.ppermute(block, axis, [(i, i ^ flip) for i in range(lax.axis_size(axi...  16.1 us
    pallas_call x2, Pallas kernels, density(): pl.pallas_call(functools.partial(density_kernel, first=first, bits=bits,...  15.3 us
    pallas_call x1, Pallas kernels, lags(): pl.pallas_call(functools.partial(lags_kernel, blocks=len(parts), frames=f...  5.16 us
    another operation x1, local copies, waits for them, and re-layouts  1.33 us
  transfers between devices with their start and end apart: 13, of which 8 were waited for; matrix products, arithmetic and copies ran while one was open for 0% of the time, Pallas kernels for 13%

profile of v1, /device:TPU:0, one launch (start us, length us, event | category | flops | bytes accessed | tf_op | source)
XLA Modules:
  0.0 62.8 jit_solution(16406960443797766323)
XLA Ops:
  0.0 0.8 %fusion = f32[1536]{0:T(1024)S(1)} fusion(f32[2]{0:T(128)} %param.8, s32[1536]{0:T(1024)} %param.7), kind=kLoop, calls=%fused_computation.7 | loop fusion | flops 7680 | bytes 12296 | tf_op jit(solution)/shard_map/reduce_sum | solution.py:305
  0.8 1.3 %constant_dynamic-slice_fusion = (f32[32,3,1536]{2,0,1:T(8,128)S(1)}, f32[32,3,1536]{2,0,1:T(8,128)S(1)}) fusion(f32[64,3,1536]{2,0,1:T(8,128)} %param.6, s32[]{:T(128)S(6)} %select_n.12, s32[]{:T(128)S(6)} %select_n.10), kind=kLoop, calls=%fused_computation.9 | loop fusion | bytes 2359304 | tf_op jit(solution)/shard_map/dynamic-slice.1
  2.3 0.5 collective-permute-start
  2.8 1.7 %collective-permute-done.sibling_ref = f32[104,1536]{1,0:T(8,128)S(1)} collective-permute-done((f32[104,1536]{1,0:T(8,128)S(1)}, f32[104,1536]{1,0:T(8,128)S(1)}, u32[]{:S(2)}, u32[]{:S(2)}) %collective-permute-start) | collective-permute-done | bytes 639008 | tf_op jit(solution)/shard_map/ppermute | solution.py:290
  4.5 7.7 %density.3 = (f32[16,4,8,128]{3,2,1,0:T(8,128)S(1)}, f32[16,4,8,128]{3,2,1,0:T(8,128)S(1)}) custom-call(s32[1]{0:T(128)} %bitcast.1.me_ref, s32[3,16]{1,0:T(4,128)S(1)} %copy-done.1, f32[104,1536]{1,0:T(8,128)S(1)} %get-tuple-element.24.own_ref, f32[104,1536]{1,0:T(8,128)S(1)} %collective-permute-done.sibling_ref), custom_call_target="tpu_custom_call" | custom-call | flops 6442450944 | bytes 524288 | tf_op jit(solution)/shard_map/density/pallas_call | solution.py:157
  12.2 3.0 %collective-permute-start.4 = (f32[16,4,8,128]{3,2,1,0:T(8,128)S(1)}, f32[16,4,8,128]{3,2,1,0:T(8,128)S(1)}, u32[]{:S(2)}, u32[]{:S(2)}) collective-permute-start(f32[16,4,8,128]{3,2,1,0:T(8,128)S(1)} %get-tuple-element.18), channel_id=1, source_target_pairs={{0,2},{1,3},{2,0},{3,1},{4,6},{5,7},{6,4},{7,5},{8,10},{9,11},{10,... | collective-permute-start | bytes 786440 | tf_op jit(solution)/shard_map/ppermute | solution.py:290
  15.2 7.7 %density.2 = (f32[16,4,8,128]{3,2,1,0:T(8,128)S(1)}, f32[16,4,8,128]{3,2,1,0:T(8,128)S(1)}) custom-call(s32[1]{0:T(128)} %bitcast.1.me_ref, s32[3,16]{1,0:T(4,128)S(1)} %copy-done.1, f32[104,1536]{1,0:T(8,128)S(1)} %get-tuple-element.24.own_ref, f32[104,1536]{1,0:T(8,128)S(1)} %collective-permute-done.sibling_ref), custom_call_target="tpu_custom_call" | custom-call | flops 6442450944 | bytes 524288 | tf_op jit(solution)/shard_map/density/pallas_call | solution.py:157
  23.0 3.1 %collective-permute-start.5 = (f32[16,2,8,128]{3,2,1,0:T(8,128)S(1)}, f32[16,2,8,128]{3,2,1,0:T(8,128)S(1)}, u32[]{:S(2)}, u32[]{:S(2)}) collective-permute-start(f32[16,2,8,128]{3,2,1,0:T(8,128)S(1)} %slice_add_fusion), channel_id=1, source_target_pairs={{0,4},{1,5},{2,6},{3,7},{4,0},{5,1},{6,2},{7,3},{8,12},{9,13},{10,... | collective-permute-start | bytes 393224 | tf_op jit(solution)/shard_map/ppermute | solution.py:290
  26.1 7.7 %collective-permute-done.1.refs_1_ = f32[16,4,8,128]{3,2,1,0:T(8,128)S(1)} collective-permute-done((f32[16,4,8,128]{3,2,1,0:T(8,128)S(1)}, f32[16,4,8,128]{3,2,1,0:T(8,128)S(1)}, u32[]{:S(2)}, u32[]{:S(2)}) %collective-permute-start.1) | collective-permute-done | bytes 262176 | tf_op jit(solution)/shard_map/ppermute | solution.py:290
  33.8 1.0 %collective-permute-start.2 = (f32[16,2,8,128]{3,2,1,0:T(8,128)S(1)}, f32[16,2,8,128]{3,2,1,0:T(8,128)S(1)}, u32[]{:S(2)}, u32[]{:S(2)}) collective-permute-start(f32[16,2,8,128]{3,2,1,0:T(8,128)S(1)} %slice_add_fusion.1), channel_id=1, source_target_pairs={{0,4},{1,5},{2,6},{3,7},{4,0},{5,1},{6,2},{7,3},{8,12},{9,13},{10,... | collective-permute-start | bytes 393224 | tf_op jit(solution)/shard_map/ppermute | solution.py:290
  34.8 0.3 waves.3
  35.2 6.6 %collective-permute-done.2.refs_2_ = f32[16,2,8,128]{3,2,1,0:T(8,128)S(1)} collective-permute-done((f32[16,2,8,128]{3,2,1,0:T(8,128)S(1)}, f32[16,2,8,128]{3,2,1,0:T(8,128)S(1)}, u32[]{:S(2)}, u32[]{:S(2)}) %collective-permute-start.2) | collective-permute-done | bytes 131104 | tf_op jit(solution)/shard_map/ppermute | solution.py:290
  41.8 0.3 waves.2
  42.2 2.5 %collective-permute-start.12 = (f32[2,8,16,128]{3,2,1,0:T(8,128)S(1)}, f32[2,8,16,128]{3,2,1,0:T(8,128)S(1)}, u32[]{:S(2)}, u32[]{:S(2)}) collective-permute-start(f32[2,8,16,128]{3,2,1,0:T(8,128)S(1)} %pad_maximum_fusion.3.refs_1_), channel_id=1, source_target_pairs={{0,24},{8,16},{16,8},{24,0},{1,25},{9,17},{17,9},{25,1},{2,26},{10... | collective-permute-start | bytes 393224 | tf_op jit(solution)/shard_map/ppermute | solution.py:290
  44.7 0.6 collective-permute-start.10
  45.3 0.5 collective-permute-start.8
  45.8 2.5 %collective-permute-start.11 = (f32[2,8,16,128]{3,2,1,0:T(8,128)S(1)}, f32[2,8,16,128]{3,2,1,0:T(8,128)S(1)}, u32[]{:S(2)}, u32[]{:S(2)}) collective-permute-start(f32[2,8,16,128]{3,2,1,0:T(8,128)S(1)} %pad_maximum_fusion.2.refs_0_), channel_id=1, source_target_pairs={{0,24},{8,16},{16,8},{24,0},{1,25},{9,17},{17,9},{25,1},{2,26},{10... | collective-permute-start | bytes 393224 | tf_op jit(solution)/shard_map/ppermute | solution.py:290
  48.3 0.6 collective-permute-start.9
  48.9 0.5 collective-permute-done.12.refs_7_
  49.4 1.7 %collective-permute-start.7 = (f32[2,8,16,128]{3,2,1,0:T(8,128)S(1)}, f32[2,8,16,128]{3,2,1,0:T(8,128)S(1)}, u32[]{:S(2)}, u32[]{:S(2)}) collective-permute-start(f32[2,8,16,128]{3,2,1,0:T(8,128)S(1)} %pad_maximum_fusion.2.refs_0_), channel_id=1, source_target_pairs={{0,8},{8,0},{16,24},{24,16},{1,9},{9,1},{17,25},{25,17},{2,10},{10... | collective-permute-start | bytes 393224 | tf_op jit(solution)/shard_map/ppermute | solution.py:290
  51.1 1.5 %collective-permute-done.10.refs_5_ = f32[2,8,16,128]{3,2,1,0:T(8,128)S(1)} collective-permute-done((f32[2,8,16,128]{3,2,1,0:T(8,128)S(1)}, f32[2,8,16,128]{3,2,1,0:T(8,128)S(1)}, u32[]{:S(2)}, u32[]{:S(2)}) %collective-permute-start.10) | collective-permute-done | bytes 131104 | tf_op jit(solution)/shard_map/ppermute | solution.py:290
  52.7 2.8 %collective-permute-done.11.refs_6_ = f32[2,8,16,128]{3,2,1,0:T(8,128)S(1)} collective-permute-done((f32[2,8,16,128]{3,2,1,0:T(8,128)S(1)}, f32[2,8,16,128]{3,2,1,0:T(8,128)S(1)}, u32[]{:S(2)}, u32[]{:S(2)}) %collective-permute-start.11) | collective-permute-done | bytes 131104 | tf_op jit(solution)/shard_map/ppermute | solution.py:290
  55.4 2.1 %collective-permute-done.9.refs_4_ = f32[2,8,16,128]{3,2,1,0:T(8,128)S(1)} collective-permute-done((f32[2,8,16,128]{3,2,1,0:T(8,128)S(1)}, f32[2,8,16,128]{3,2,1,0:T(8,128)S(1)}, u32[]{:S(2)}, u32[]{:S(2)}) %collective-permute-start.9) | collective-permute-done | bytes 131104 | tf_op jit(solution)/shard_map/ppermute | solution.py:290
  57.7 5.2 %lags.1 = f32[512,128]{1,0:T(8,128)} custom-call(s32[2]{0:T(128)S(1)} %pad_add_fusion.place_ref, s32[3,16]{1,0:T(4,128)S(1)} %copy-done.1, s32[1,128]{1,0:T(1,128)S(1)} %bitcast.15, bf16[320,768]{1,0:T(8,128)(2,1)S(1)} %copy-done, f32[2,8,16,128]{3,2,1,0:T(8,128)S(1)} %pad_maximum_fusion.2.refs_0_, f32[2,8,16,128]{3,2,1,0:T(8,128)S(1)} %pad_maximum_fusion.3.refs_1_, ...), custom_call_target="tpu_custom_call" | custom-call | tf_op jit(solution)/shard_map/lags/pallas_call | solution.py:278
  (22 shorter events, 0.7 us)
Async XLA Ops:
  2.2 2.3 %copy-start.1 = (s32[3,16]{1,0:T(4,128)S(1)}, s32[3,16]{1,0:T(4,128)}, u32[]{:S(2)}) copy-start(s32[3,16]{1,0:T(4,128)} %wave_ref.5) | copy-start | bytes 580
  2.3 2.2 %collective-permute-start = (f32[104,1536]{1,0:T(8,128)S(1)}, f32[104,1536]{1,0:T(8,128)S(1)}, u32[]{:S(2)}, u32[]{:S(2)}) collective-permute-start(f32[104,1536]{1,0:T(8,128)S(1)} %get-tuple-element.23), channel_id=1, source_target_pairs={{0,1},{1,0},{2,3},{3,2},{4,5},{5,4},{6,7},{7,6},{8,9},{9,8},{10,11... | collective-permute-start | bytes 1916936 | tf_op jit(solution)/shard_map/ppermute | solution.py:290
  12.2 10.8 %collective-permute-start.4 = (f32[16,4,8,128]{3,2,1,0:T(8,128)S(1)}, f32[16,4,8,128]{3,2,1,0:T(8,128)S(1)}, u32[]{:S(2)}, u32[]{:S(2)}) collective-permute-start(f32[16,4,8,128]{3,2,1,0:T(8,128)S(1)} %get-tuple-element.18), channel_id=1, source_target_pairs={{0,2},{1,3},{2,0},{3,1},{4,6},{5,7},{6,4},{7,5},{8,10},{9,11},{10,... | collective-permute-start | bytes 786440 | tf_op jit(solution)/shard_map/ppermute | solution.py:290
  22.9 11.0 %collective-permute-start.1 = (f32[16,4,8,128]{3,2,1,0:T(8,128)S(1)}, f32[16,4,8,128]{3,2,1,0:T(8,128)S(1)}, u32[]{:S(2)}, u32[]{:S(2)}) collective-permute-start(f32[16,4,8,128]{3,2,1,0:T(8,128)S(1)} %get-tuple-element.14), channel_id=1, source_target_pairs={{0,2},{1,3},{2,0},{3,1},{4,6},{5,7},{6,4},{7,5},{8,10},{9,11},{10,... | collective-permute-start | bytes 786440 | tf_op jit(solution)/shard_map/ppermute | solution.py:290
  23.0 34.7 %copy-start = (bf16[320,768]{1,0:T(8,128)(2,1)S(1)}, bf16[320,768]{1,0:T(8,128)(2,1)}, u32[]{:S(2)}) copy-start(bf16[320,768]{1,0:T(8,128)(2,1)} %constant.20.clone.basis_ref) | copy-start | bytes 1474564
  23.0 34.7 %copy-start.2 = (s32[128]{0:T(128)S(1)}, s32[128]{0:T(128)}, u32[]{:S(2)}) copy-start(s32[128]{0:T(128)} %param.10) | copy-start | bytes 1540
  23.0 11.8 %collective-permute-start.5 = (f32[16,2,8,128]{3,2,1,0:T(8,128)S(1)}, f32[16,2,8,128]{3,2,1,0:T(8,128)S(1)}, u32[]{:S(2)}, u32[]{:S(2)}) collective-permute-start(f32[16,2,8,128]{3,2,1,0:T(8,128)S(1)} %slice_add_fusion), channel_id=1, source_target_pairs={{0,4},{1,5},{2,6},{3,7},{4,0},{5,1},{6,2},{7,3},{8,12},{9,13},{10,... | collective-permute-start | bytes 393224 | tf_op jit(solution)/shard_map/ppermute | solution.py:290
  33.8 8.0 %collective-permute-start.2 = (f32[16,2,8,128]{3,2,1,0:T(8,128)S(1)}, f32[16,2,8,128]{3,2,1,0:T(8,128)S(1)}, u32[]{:S(2)}, u32[]{:S(2)}) collective-permute-start(f32[16,2,8,128]{3,2,1,0:T(8,128)S(1)} %slice_add_fusion.1), channel_id=1, source_target_pairs={{0,4},{1,5},{2,6},{3,7},{4,0},{5,1},{6,2},{7,3},{8,12},{9,13},{10,... | collective-permute-start | bytes 393224 | tf_op jit(solution)/shard_map/ppermute | solution.py:290
  35.1 7.1 %collective-permute-start.6 = (f32[8,16,128]{2,1,0:T(8,128)S(1)}, f32[8,16,128]{2,1,0:T(8,128)S(1)}, u32[]{:S(2)}, u32[]{:S(2)}) collective-permute-start(f32[8,16,128]{2,1,0:T(8,128)S(1)} %get-tuple-element.20), channel_id=1, source_target_pairs={{0,1},{1,0},{2,3},{3,2},{4,5},{5,4},{6,7},{7,6},{8,9},{9,8},{10,11... | collective-permute-start | bytes 196616 | tf_op jit(solution)/shard_map/ppermute | solution.py:290
  42.1 3.7 %collective-permute-start.3 = (f32[8,16,128]{2,1,0:T(8,128)S(1)}, f32[8,16,128]{2,1,0:T(8,128)S(1)}, u32[]{:S(2)}, u32[]{:S(2)}) collective-permute-start(f32[8,16,128]{2,1,0:T(8,128)S(1)} %get-tuple-element.16), channel_id=1, source_target_pairs={{0,1},{1,0},{2,3},{3,2},{4,5},{5,4},{6,7},{7,6},{8,9},{9,8},{10,11... | collective-permute-start | bytes 196616 | tf_op jit(solution)/shard_map/ppermute | solution.py:290
  42.2 7.2 %collective-permute-start.12 = (f32[2,8,16,128]{3,2,1,0:T(8,128)S(1)}, f32[2,8,16,128]{3,2,1,0:T(8,128)S(1)}, u32[]{:S(2)}, u32[]{:S(2)}) collective-permute-start(f32[2,8,16,128]{3,2,1,0:T(8,128)S(1)} %pad_maximum_fusion.3.refs_1_), channel_id=1, source_target_pairs={{0,24},{8,16},{16,8},{24,0},{1,25},{9,17},{17,9},{25,1},{2,26},{10... | collective-permute-start | bytes 393224 | tf_op jit(solution)/shard_map/ppermute | solution.py:290
  44.7 7.9 %collective-permute-start.10 = (f32[2,8,16,128]{3,2,1,0:T(8,128)S(1)}, f32[2,8,16,128]{3,2,1,0:T(8,128)S(1)}, u32[]{:S(2)}, u32[]{:S(2)}) collective-permute-start(f32[2,8,16,128]{3,2,1,0:T(8,128)S(1)} %pad_maximum_fusion.3.refs_1_), channel_id=1, source_target_pairs={{0,16},{8,24},{16,0},{24,8},{1,17},{9,25},{17,1},{25,9},{2,18},{10... | collective-permute-start | bytes 393224 | tf_op jit(solution)/shard_map/ppermute | solution.py:290
  45.3 7.4 %collective-permute-start.8 = (f32[2,8,16,128]{3,2,1,0:T(8,128)S(1)}, f32[2,8,16,128]{3,2,1,0:T(8,128)S(1)}, u32[]{:S(2)}, u32[]{:S(2)}) collective-permute-start(f32[2,8,16,128]{3,2,1,0:T(8,128)S(1)} %pad_maximum_fusion.3.refs_1_), channel_id=1, source_target_pairs={{0,8},{8,0},{16,24},{24,16},{1,9},{9,1},{17,25},{25,17},{2,10},{10... | collective-permute-start | bytes 393224 | tf_op jit(solution)/shard_map/ppermute | solution.py:290
  45.8 9.6 %collective-permute-start.11 = (f32[2,8,16,128]{3,2,1,0:T(8,128)S(1)}, f32[2,8,16,128]{3,2,1,0:T(8,128)S(1)}, u32[]{:S(2)}, u32[]{:S(2)}) collective-permute-start(f32[2,8,16,128]{3,2,1,0:T(8,128)S(1)} %pad_maximum_fusion.2.refs_0_), channel_id=1, source_target_pairs={{0,24},{8,16},{16,8},{24,0},{1,25},{9,17},{17,9},{25,1},{2,26},{10... | collective-permute-start | bytes 393224 | tf_op jit(solution)/shard_map/ppermute | solution.py:290
  48.3 9.2 %collective-permute-start.9 = (f32[2,8,16,128]{3,2,1,0:T(8,128)S(1)}, f32[2,8,16,128]{3,2,1,0:T(8,128)S(1)}, u32[]{:S(2)}, u32[]{:S(2)}) collective-permute-start(f32[2,8,16,128]{3,2,1,0:T(8,128)S(1)} %pad_maximum_fusion.2.refs_0_), channel_id=1, source_target_pairs={{0,16},{8,24},{16,0},{24,8},{1,17},{9,25},{17,1},{25,9},{2,18},{10... | collective-permute-start | bytes 393224 | tf_op jit(solution)/shard_map/ppermute | solution.py:290
  49.4 8.3 %collective-permute-start.7 = (f32[2,8,16,128]{3,2,1,0:T(8,128)S(1)}, f32[2,8,16,128]{3,2,1,0:T(8,128)S(1)}, u32[]{:S(2)}, u32[]{:S(2)}) collective-permute-start(f32[2,8,16,128]{3,2,1,0:T(8,128)S(1)} %pad_maximum_fusion.2.refs_0_), channel_id=1, source_target_pairs={{0,8},{8,0},{16,24},{24,16},{1,9},{9,1},{17,25},{25,17},{2,10},{10... | collective-permute-start | bytes 393224 | tf_op jit(solution)/shard_map/ppermute | solution.py:290

commit v2 on v1

v2 whole, which is shorter than its diff:
```python
import functools
import math

import jax
import jax.numpy as jnp
import numpy as np
from jax import lax
from jax.experimental import pallas as pl
from jax.experimental.pallas import tpu as pltpu
from jax.sharding import PartitionSpec as P

COS = (1.0, -19.73920440673828, 64.93911743164062, -85.45014190673828, 60.16762924194336, -25.967599868774414, 6.528658390045166)
SIN = (6.2831854820251465, -41.34170150756836, 81.60513305664062, -76.70301818847656, 42.02592849731445, -14.899847030639648, 3.2381374835968018)

SIZES = (2, 1, 1)
RINGS = ((0,), (1, 2))
TIES = ((2, 0),)
PITCH = 17
WIDE = 33
VMEM_LIMIT = 48 << 20


def polynomial(coefficients, s):
    value = coefficients[-1] * s + coefficients[-2]
    for c in coefficients[-3::-1]:
        value = value * s + c
    return value


def circle(turns):
    r = turns - jnp.round(turns)
    s = r * r
    return polynomial(COS, s), polynomial(SIN, s) * r


def tables(x, y, z, weight, put_x, put_y, put_z):
    c, s = circle(0.5 * x)
    twice = 4.0 * c * c - 2.0
    before, now = (c, -s), (c, s)
    for m in range(8):
        put_x(m, now[0])
        put_x(8 + m, now[1])
        before, now = now, tuple(twice * p - q for p, q in zip(now, before))
    c, s = circle(0.5 * y)
    twice = 4.0 * c * c - 2.0
    for l, value in enumerate((c, s, (twice - 1.0) * c, (twice + 1.0) * s)):
        put_y(l, value)
    c2 = 0.5 * twice * twice - 1.0
    s2 = 2.0 * twice * s * c
    four = 4.0 * c2 * c2
    for h, value in enumerate((c2, s2, c2 * (four - 3.0), s2 * (four - 1.0))):
        put_y(4 + h, value)
    real, imag = circle(8.5 * (x + y))
    c, s = circle(z)
    twice = c + c
    before, now = (weight, jnp.zeros_like(weight)), (weight * c, weight * s)
    for k in range(16):
        c, s = (value.astype(jnp.bfloat16).astype(jnp.float32) for value in now)
        put_z(k, real * c - imag * s)
        put_z(16 + k, real * s + imag * c)
        before, now = now, tuple(twice * p - q for p, q in zip(now, before))


def split(value):
    high = value.astype(jnp.bfloat16)
    return high, (value - high.astype(jnp.float32)).astype(jnp.bfloat16)


def slot_of(k):
    return jnp.where(k >= 9, k - 9, 16 - k)


def turned(value, quarter):
    return pltpu.roll(value, 64, 1) * quarter


def density_kernel(
    me_ref, wave_ref, length_ref, own_ref, sibling_ref, own_label, sibling_label, keep_ref, send_ref, *scratch, groups, bits, shift
):
    xs, ys, zs, prod, grid = scratch
    sources = ((own_ref, own_label), (sibling_ref, sibling_label))
    rows = own_ref.shape[0] // 3
    tiles = own_ref.shape[1] // 128

    def fill(g, source, j):
        ref, label_ref = sources[source]
        base = pl.multiple_of(g * 8, 8)
        lanes = pl.ds(pl.multiple_of(j * 128, 128), 128)
        x, y, z = (ref[pl.ds(base + rows * axis, 8), lanes] for axis in range(3))
        label = jnp.broadcast_to(label_ref[:, lanes], (8, 128))
        weight = jnp.zeros((8, 128), jnp.float32)
        for kind in range(length_ref.shape[0]):
            weight = weight + jnp.where(label == kind, length_ref[kind], 0.0)

        def put(table, pitch):
            def go(f, value):
                table[source * tiles + j, pl.ds(f, 8, stride=pitch), :] = value

            return go

        tables(x, y, z, weight, put(xs, PITCH), put(ys, PITCH), put(zs, WIDE))

    def one_frame(f, carry):
        r0 = f * PITCH
        total = jnp.zeros((128, 128), jnp.float32)
        for pair in range(tiles):
            left, right = [], []
            for t in (2 * pair, 2 * pair + 1):
                x = xs[t, pl.ds(r0, 16), :]
                z = zs[t, pl.ds(f * WIDE, 32), :]
                exact = jnp.concatenate([x * ys[t, pl.ds(r0 + l, 1), :] for l in range(4)], 0)
                left.append(jnp.concatenate(split(exact), 0))
                hs = [ys[t, pl.ds(r0 + 4 + h, 1), :] for h in range(4)]
                right.append(jnp.concatenate([part * h for part in (z[:16], z[16:]) for h in hs], 0).astype(jnp.bfloat16))
            total = total + lax.dot_general(
                jnp.concatenate(left, 1),
                jnp.concatenate(right, 1),
                (((1,), (1,)), ((), ())),
                preferred_element_type=jnp.float32,
            )
        prod[f] = total[:64] + total[64:]
        return carry

    def one_group(g, carry):
        for source in range(2):

            def one_tile(j, carry):
                fill(g, source, j)
                return carry

            lax.fori_loop(0, tiles, one_tile, 0, unroll=4)
        lax.fori_loop(0, 8, one_frame, 0, unroll=8)
        collect(g, me_ref, wave_ref, keep_ref, send_ref, prod, grid, bits, shift)
        return carry

    lax.fori_loop(0, groups, one_group, 0)


def collect(g, me_ref, wave_ref, keep_ref, send_ref, prod, grid, bits, shift):
    lane = lax.broadcasted_iota(jnp.int32, (8, 128), 1)
    quarter = jnp.where(lane < 64, -1.0, 1.0).astype(jnp.float32)
    for f in range(8):
        for l in range(4):
            cosine = prod[f, l * 16 : l * 16 + 8, :]
            sine = turned(prod[f, l * 16 + 8 : l * 16 + 16, :], quarter)
            r = (f * 4 + l) * PITCH
            grid[r : r + 8, :] = cosine + sine
            grid[r + 8 : r + 16, :] = cosine - sine

    me = me_ref[0]
    for i in range(8):
        flip = sum(((i >> (2 - j)) & 1) << bit for j, bit in enumerate(bits))
        pair = (me ^ flip) >> shift
        out_ref = keep_ref if i < 4 else send_ref
        for j in range(2):
            slot = slot_of(wave_ref[0, 2 * pair + j])
            for f in range(8):
                out_ref[g * 8 + f, i % 4, 4 * j : 4 * j + 4, :] = grid[pl.ds(f * 4 * PITCH + slot, 4, stride=PITCH), :]


def density(me, wave_numbers, lengths, own, sibling, own_label, sibling_label, groups, bits, shift):
    tiles = own.shape[1] // 128
    frames = groups * 8
    shape = jax.ShapeDtypeStruct((frames, 4, 8, 128), jnp.float32)
    smem, vmem = (pl.BlockSpec(memory_space=space) for space in (pltpu.SMEM, pltpu.VMEM))
    tables_shapes = [pltpu.VMEM((2 * tiles, 8 * pitch, 128), jnp.float32) for pitch in (PITCH, PITCH, WIDE)]
    return pl.pallas_call(
        functools.partial(density_kernel, groups=groups, bits=bits, shift=shift),
        out_shape=(shape, shape),
        in_specs=[smem] * 3 + [vmem] * 4,
        out_specs=(vmem, vmem),
        scratch_shapes=tables_shapes + [pltpu.VMEM((8, 64, 128), jnp.float32), pltpu.VMEM((32 * PITCH, 128), jnp.float32)],
        compiler_params=pltpu.CompilerParams(vmem_limit_bytes=VMEM_LIMIT),
        cost_estimate=pl.CostEstimate(flops=frames * tiles * 128 * 128 * 128 * 2 * 8, bytes_accessed=frames * 32768, transcendentals=0),
        name="density",
    )(me, wave_numbers, lengths, own, sibling, own_label, sibling_label)


def combine(value, swap, second, quarter):
    mixed = jnp.where(second, turned(value, quarter), value)
    return swap(mixed) + jnp.where(second, -mixed, mixed)


def waves_kernel(*refs, terms):
    parts, outs = refs[:terms], refs[terms:]
    frames = parts[0].shape[0]
    row = lax.broadcasted_iota(jnp.int32, (8, 128), 0)
    lane = lax.broadcasted_iota(jnp.int32, (8, 128), 1)
    quarter = jnp.where(lane < 64, -1.0, 1.0).astype(jnp.float32)
    bit_l, bit_h = (row & 1) == 1, (lane & 16) == 16

    def swap(axis, distance, second):
        size = (8, 128)[axis]

        def go(value):
            return jnp.where(second, pltpu.roll(value, distance, axis), pltpu.roll(value, size - distance, axis))

        return go

    for g, out in enumerate(outs):
        for t in range(frames):
            value = parts[0][t, g]
            for part in parts[1:]:
                value = value + part[t, g]
            value = combine(value, swap(0, 1, bit_l), bit_l, quarter)
            value = combine(value, swap(1, 16, bit_h), bit_h, quarter)
            out[:, t, :] = value


def waves(parts, groups):
    frames = parts[0].shape[0]
    shape = jax.ShapeDtypeStruct((8, frames, 128), jnp.float32)
    return pl.pallas_call(
        functools.partial(waves_kernel, terms=len(parts)),
        grid=(1,),
        out_shape=(shape,) * groups,
        in_specs=[pl.BlockSpec((frames, groups, 8, 128), lambda g: (0, 0, 0, 0))] * len(parts),
        out_specs=(pl.BlockSpec((8, frames, 128), lambda g: (0, 0, 0)),) * groups,
        compiler_params=pltpu.CompilerParams(vmem_limit_bytes=VMEM_LIMIT),
        name="waves",
    )(*parts)


def lags_kernel(place_ref, wave_ref, lag_ref, basis_ref, *refs, blocks, frames, atoms, period, share):
    parts, (out_ref, series, result) = refs[:blocks], refs[blocks:]
    half = period // 2
    tm, me = place_ref[0], place_ref[1]
    steps = blocks // len(RINGS)
    per_block = frames // steps
    at = 0
    for ring in range(len(RINGS)):
        size = parts[ring * steps].shape[2]
        for p in range(steps):
            for side in range(2):
                start = (tm ^ p) * per_block + ((me & 1) ^ side) * (per_block // 2) + at
                series[:, pl.ds(pl.multiple_of(start, 8), size), :] = parts[ring * steps + p][side]
        at += size
    lane = lax.broadcasted_iota(jnp.int32, (8, 128), 1)
    source = lane
    for n in range(16):
        source = jnp.where((lane & 15) == n, lane - n + wave_ref[2, n] - 1, source)
    count = lag_ref.shape[1]
    order = 2 * lax.broadcasted_iota(jnp.int32, (count, half), 1) + 1
    lag = jnp.broadcast_to(lag_ref[...], (half, count)).T
    phase = (order * lag).astype(jnp.float32)
    turns = phase - jnp.round(phase * (0.5 / period)) * (2.0 * period)
    cosine, _ = circle(turns * (0.5 / period))
    scale = (2.0 / period) / ((frames - lag).astype(jnp.float32) * float(atoms))
    high, low = split(cosine * scale)
    weights = jnp.concatenate([high, low, high], 1)
    powers = []
    for l in range(4):
        high, low = split(jnp.concatenate([series[l], series[4 + l]], 1))
        spectrum = jnp.dot(basis_ref[...], jnp.concatenate([high, high, low], 0), preferred_element_type=jnp.float32)
        power = spectrum[:half] * spectrum[:half] + spectrum[half:] * spectrum[half:]
        powers.append(
            jnp.concatenate(
                [
                    jnp.where(
                        lane < 64,
                        power[i : i + 8, :128] + pltpu.roll(power[i : i + 8, :128], 64, 1),
                        power[i : i + 8, 128:] + pltpu.roll(power[i : i + 8, 128:], 64, 1),
                    )
                    for i in range(0, half, 8)
                ],
                0,
            )
        )
    high, low = split(jnp.concatenate(powers, 1))
    total = jnp.dot(weights, jnp.concatenate([high, high, low], 0), preferred_element_type=jnp.float32)
    for l in range(4):
        part = total[:, l * 128 : l * 128 + 128]
        part = jnp.concatenate([jnp.take_along_axis(part[i : i + 8], source, axis=1) for i in range(0, count, 8)], 0)
        result[l] = part.T

    def place_of(b):
        k = wave_ref[1, b] - 1
        h, l = (jnp.where(v == 0, 3, jnp.where(v == 1, 1, jnp.where(v == 2, 0, 2))) for v in (k // 4, k % 4))
        return l, h * 16

    rows = share // 16
    known = [place_of(b) for b in range(16)] if rows == 32 else None
    for i in range(rows):
        if known:
            a, (l, start) = i // 16, known[i % 16]
        else:
            block = (me * rows + i) % 32
            a, (l, start) = block // 16, place_of(block % 16)
        out_ref[i * 16 : i * 16 + 16, :] = result[l, pl.ds(pl.multiple_of(a * 64 + start, 16), 16), :]


def lags(place, wave_numbers, lag_list, parts, frames, atoms, period, share):
    half = period // 2
    angle = np.outer(2 * np.arange(half) + 1, np.arange(frames)) * (math.pi / period)
    basis = np.concatenate([np.cos(angle), np.sin(angle)], 0).astype(np.float32)
    high = basis.astype(jnp.bfloat16)
    low = (basis - high.astype(np.float32)).astype(jnp.bfloat16)
    basis = jnp.asarray(np.concatenate([high, low, high], 1))
    smem = pl.BlockSpec(memory_space=pltpu.SMEM)
    vmem = pl.BlockSpec(memory_space=pltpu.VMEM)
    return pl.pallas_call(
        functools.partial(lags_kernel, blocks=len(parts), frames=frames, atoms=atoms, period=period, share=share),
        out_shape=jax.ShapeDtypeStruct((share, lag_list.shape[0]), jnp.float32),
        in_specs=[smem, smem] + [vmem] * (2 + len(parts)),
        out_specs=vmem,
        scratch_shapes=[pltpu.VMEM((8, frames, 128), jnp.float32), pltpu.VMEM((4, 128, lag_list.shape[0]), jnp.float32)],
        compiler_params=pltpu.CompilerParams(vmem_limit_bytes=VMEM_LIMIT),
        name="lags",
    )(place, wave_numbers, lag_list[None, :], basis, *parts)


def swapped(block, axis, flip):
    return lax.ppermute(block, axis, [(i, i ^ flip) for i in range(lax.axis_size(axis))])


def on_device(positions, species, lengths, wave_numbers, lag_list):
    frames, _, atoms = positions.shape
    devices, blocks = lax.axis_size("atom"), lax.axis_size("tm")
    me, tm = lax.axis_index("atom"), lax.axis_index("tm")
    share = wave_numbers.shape[1] ** 3 // devices
    period = (frames * blocks * 5) // 4
    half = frames // 2
    shift = devices.bit_length() - 4
    flips = [1 << bit for bit in range(1, devices.bit_length() - 1)]
    bits = ([bit for bit in range(1, devices.bit_length() - 1) if bit >= shift] + [0])[:3]

    turned_positions = jnp.transpose(positions, (1, 0, 2))
    sizes = [size * 8 for size in SIZES]

    def payload(core, start, size):
        part = lax.dynamic_slice_in_dim(turned_positions, core * half + start, size, 1)
        return part.reshape(3 * size, atoms)

    labels = [species[None, :], swapped(species, "atom", 1)[None, :]]
    place = jnp.stack([tm, me]).astype(jnp.int32)
    finals, rings = [], []
    for c, size in enumerate(sizes):
        start = sum(sizes[:c])
        own = payload(me & 1, start, size)
        sibling = swapped(payload(1 - (me & 1), start, size), "atom", 1)
        keep, send = density(place[1:2], wave_numbers, lengths, own, sibling, *labels, size // 8, bits, shift)
        terms, fresh, held = [keep], True, 8
        for flip in flips:
            if flip >= (1 << shift):
                held //= 2
                out = send if fresh else sum(t[:, held : 2 * held] for t in terms)
                fresh = False
                terms = terms + [swapped(out, "atom", flip)]
            else:
                keep, send = (a + swapped(a, "atom", flip) for a in (keep, send))
                terms = [keep]
        for chunk, ring in TIES:
            if chunk == c:
                terms[-1], *rings[ring][1:] = lax.optimization_barrier((terms[-1], *rings[ring][1:]))
        final = waves(terms, held)
        finals.append((final[0], final[-1]))
        for ring in RINGS:
            if ring[-1] == c:
                mine, other = (jnp.concatenate([finals[i][j] for i in ring], 1) for j in range(2))
                both = jnp.stack([mine, swapped(other, "atom", 1)])
                rings.append([both] + [swapped(both, "tm", p) for p in range(1, blocks)])
    parts = [part for ring in rings for part in ring]
    return lags(place, wave_numbers, lag_list, parts, frames * blocks, atoms * devices, period, share)


def solution(mesh):
    placed = (P("tm", None, "atom"), P("atom"), P(), P(), P())
    return jax.shard_map(
        on_device, mesh=mesh, in_specs=placed, out_specs=P("atom", None), check_vma=False
    )
```

time: 63.1 us -> 54.2 us (0.86)
  waiting for transfers between devices: 23.1 us -> 15.1 us
  starting transfers between devices: 16.1 us -> 19 us
  Pallas kernels: 21.1 us -> 18.4 us
  other arithmetic: 1.02 us -> 0.15 us
    ppermute x13 -> x18, waiting for transfers between devices: 23.1 us -> 15.1 us  [swapped(): lax.ppermute(block, axis, [(i, i ^ flip) for i in range(lax.axis_size(axi...]
    ppermute x13 -> x18, starting transfers between devices: 16.1 us -> 19 us  [swapped(): lax.ppermute(block, axis, [(i, i ^ flip) for i in range(lax.axis_size(axi...]
    pallas_call x1, Pallas kernels: 5.16 us -> 2.56 us  [lags(): pl.pallas_call(functools.partial(lags_kernel, blocks=len(parts), frames=f...]
    reduce_sum x1 -> x0, other arithmetic: 0.8 us -> none  [on_device(): jnp.sum(jnp.where(species[None, :] == labels[:, None], lengths[:, None],...]
    pallas_call x2 -> x3, Pallas kernels: 15.3 us -> 15 us  [density(): pl.pallas_call(functools.partial(density_kernel, groups=groups, bits=bits...]
  transfers between devices with their start and end apart: 13 -> 18, of which waited for: 8 -> 9; matrix products, arithmetic and copies ran while one was open for 0% -> 0% of each run, Pallas kernels for 13% -> 29%
where the time goes in v2:
time: 54.2 us; the launch traced here: 54.1 us
  starting transfers between devices  19 us (35%)
  Pallas kernels  18.4 us (34%)
  waiting for transfers between devices  15.1 us (28%)
  local copies, waits for them, and re-layouts  1.28 us (2%)
    ppermute x18, starting transfers between devices, swapped(): lax.ppermute(block, axis, [(i, i ^ flip) for i in range(lax.axis_size(axi...  19 us
    ppermute x18, waiting for transfers between devices, swapped(): lax.ppermute(block, axis, [(i, i ^ flip) for i in range(lax.axis_size(axi...  15.1 us
    pallas_call x3, Pallas kernels, density(): pl.pallas_call(functools.partial(density_kernel, groups=groups, bits=bits...  15 us
    pallas_call x1, Pallas kernels, lags(): pl.pallas_call(functools.partial(lags_kernel, blocks=len(parts), frames=f...  2.56 us
    another operation x1, local copies, waits for them, and re-layouts  1.2 us
  transfers between devices with their start and end apart: 18, of which 9 were waited for; matrix products, arithmetic and copies ran while one was open for 0% of the time, Pallas kernels for 29%

profile of v2, /device:TPU:0, one launch (start us, length us, event | category | flops | bytes accessed | tf_op | source)
XLA Modules:
  0.0 54.1 jit_solution(10901954272066170199)
XLA Ops:
  0.0 1.2 %constant_dynamic-slice_fusion = (f32[16,3,1536]{2,0,1:T(8,128)S(1)}, f32[16,3,1536]{2,0,1:T(8,128)S(1)}) fusion(f32[64,3,1536]{2,0,1:T(8,128)} %param.6, s32[]{:T(128)S(6)} %select_n.19, s32[]{:T(128)S(6)} %select_n.18), kind=kLoop, calls=%fused_computation.11 | loop fusion | bytes 1179656 | tf_op jit(solution)/shard_map/dynamic-slice.1
  1.2 0.5 collective-permute-start
  1.9 0.5 collective-permute-start.5
  2.5 0.5 collective-permute-done.1
  3.0 7.2 %density.3 = (f32[16,4,8,128]{3,2,1,0:T(8,128)S(1)}, f32[16,4,8,128]{3,2,1,0:T(8,128)S(1)}) custom-call(s32[1]{0:T(128)} %bitcast.1.me_ref, s32[3,16]{1,0:T(4,128)S(1)} %copy-done.1, f32[2]{0:T(128)S(1)} %copy-done.3, f32[48,1536]{1,0:T(8,128)S(1)} %bitcast.30, f32[48,1536]{1,0:T(8,128)S(1)} %collective-permute-done.sibling_ref, ...), custom_call_target="tpu_custom_call" | custom-call | flops 6442450944 | bytes 524288 | tf_op jit(solution)/shard_map/density/pallas_call | solution.py:167
  10.2 3.0 %collective-permute-start.2 = (f32[16,4,8,128]{3,2,1,0:T(8,128)S(1)}, f32[16,4,8,128]{3,2,1,0:T(8,128)S(1)}, u32[]{:S(2)}, u32[]{:S(2)}) collective-permute-start(f32[16,4,8,128]{3,2,1,0:T(8,128)S(1)} %get-tuple-element.22), channel_id=1, source_target_pairs={{0,2},{1,3},{2,0},{3,1},{4,6},{5,7},{6,4},{7,5},{8,10},{9,11},{10,... | collective-permute-start | bytes 786440 | tf_op jit(solution)/shard_map/ppermute | solution.py:313
  13.2 3.9 %density.5 = (f32[8,4,8,128]{3,2,1,0:T(8,128)S(1)}, f32[8,4,8,128]{3,2,1,0:T(8,128)S(1)}) custom-call(s32[1]{0:T(128)} %bitcast.1.me_ref, s32[3,16]{1,0:T(4,128)S(1)} %copy-done.1, f32[2]{0:T(128)S(1)} %copy-done.3, f32[24,1536]{1,0:T(8,128)S(1)} %get-tuple-element.40.own_ref, f32[24,1536]{1,0:T(8,128)S(1)} %collective-permute-done.11.sibling_ref, ...), custom_call_target="tpu_custom_call" | custom-call | flops 3221225472 | bytes 262144 | tf_op jit(solution)/shard_map/density/pallas_call | solution.py:167
  17.2 2.7 %collective-permute-done.2.refs_1_ = f32[16,4,8,128]{3,2,1,0:T(8,128)S(1)} collective-permute-done((f32[16,4,8,128]{3,2,1,0:T(8,128)S(1)}, f32[16,4,8,128]{3,2,1,0:T(8,128)S(1)}, u32[]{:S(2)}, u32[]{:S(2)}) %collective-permute-start.2) | collective-permute-done | bytes 262176 | tf_op jit(solution)/shard_map/ppermute | solution.py:313
  20.0 3.0 %collective-permute-start.3 = (f32[16,2,8,128]{3,2,1,0:T(8,128)S(1)}, f32[16,2,8,128]{3,2,1,0:T(8,128)S(1)}, u32[]{:S(2)}, u32[]{:S(2)}) collective-permute-start(f32[16,2,8,128]{3,2,1,0:T(8,128)S(1)} %slice_add_fusion), channel_id=1, source_target_pairs={{0,4},{1,5},{2,6},{3,7},{4,0},{5,1},{6,2},{7,3},{8,12},{9,13},{10,... | collective-permute-start | bytes 393224 | tf_op jit(solution)/shard_map/ppermute | solution.py:313
  23.0 3.9 %density.4 = (f32[8,4,8,128]{3,2,1,0:T(8,128)S(1)}, f32[8,4,8,128]{3,2,1,0:T(8,128)S(1)}) custom-call(s32[1]{0:T(128)} %bitcast.1.me_ref, s32[3,16]{1,0:T(4,128)S(1)} %copy-done.1, f32[2]{0:T(128)S(1)} %copy-done.3, f32[24,1536]{1,0:T(8,128)S(1)} %get-tuple-element.39.own_ref, f32[24,1536]{1,0:T(8,128)S(1)} %collective-permute-done.5.sibling_ref, ...), custom_call_target="tpu_custom_call" | custom-call | flops 3221225472 | bytes 262144 | tf_op jit(solution)/shard_map/density/pallas_call | solution.py:167
  26.9 2.2 %collective-permute-start.6 = (f32[8,4,8,128]{3,2,1,0:T(8,128)S(1)}, f32[8,4,8,128]{3,2,1,0:T(8,128)S(1)}, u32[]{:S(2)}, u32[]{:S(2)}) collective-permute-start(f32[8,4,8,128]{3,2,1,0:T(8,128)S(1)} %get-tuple-element.26), channel_id=1, source_target_pairs={{0,2},{1,3},{2,0},{3,1},{4,6},{5,7},{6,4},{7,5},{8,10},{9,11},{10,... | collective-permute-start | bytes 393224 | tf_op jit(solution)/shard_map/ppermute | solution.py:313
  29.9 0.8 %collective-permute-done.4 = f32[8,16,128]{2,1,0:T(8,128)S(1)} collective-permute-done((f32[8,16,128]{2,1,0:T(8,128)S(1)}, f32[8,16,128]{2,1,0:T(8,128)S(1)}, u32[]{:S(2)}, u32[]{:S(2)}) %collective-permute-start.4) | collective-permute-done | bytes 65568 | tf_op jit(solution)/shard_map/ppermute | solution.py:313
  30.7 1.6 %collective-permute-start.8 = (f32[2,8,16,128]{3,2,1,0:T(8,128)S(1)}, f32[2,8,16,128]{3,2,1,0:T(8,128)S(1)}, u32[]{:S(2)}, u32[]{:S(2)}) collective-permute-start(f32[2,8,16,128]{3,2,1,0:T(8,128)S(1)} %pad_maximum_fusion.refs_0_), channel_id=1, source_target_pairs={{0,8},{8,0},{16,24},{24,16},{1,9},{9,1},{17,25},{25,17},{2,10},{10... | collective-permute-start | bytes 393224 | tf_op jit(solution)/shard_map/ppermute | solution.py:313
  32.3 1.5 %collective-permute-start.9 = (f32[2,8,16,128]{3,2,1,0:T(8,128)S(1)}, f32[2,8,16,128]{3,2,1,0:T(8,128)S(1)}, u32[]{:S(2)}, u32[]{:S(2)}) collective-permute-start(f32[2,8,16,128]{3,2,1,0:T(8,128)S(1)} %pad_maximum_fusion.refs_0_), channel_id=1, source_target_pairs={{0,16},{8,24},{16,0},{24,8},{1,17},{9,25},{17,1},{25,9},{2,18},{10... | collective-permute-start | bytes 393224 | tf_op jit(solution)/shard_map/ppermute | solution.py:313
  33.8 0.5 collective-permute-start.10
  34.3 1.8 %collective-permute-start.7 = (f32[8,2,8,128]{3,2,1,0:T(8,128)S(1)}, f32[8,2,8,128]{3,2,1,0:T(8,128)S(1)}, u32[]{:S(2)}, u32[]{:S(2)}) collective-permute-start(f32[8,2,8,128]{3,2,1,0:T(8,128)S(1)} %slice_add_fusion.2), channel_id=1, source_target_pairs={{0,4},{1,5},{2,6},{3,7},{4,0},{5,1},{6,2},{7,3},{8,12},{9,13},{10,... | collective-permute-start | bytes 196616 | tf_op jit(solution)/shard_map/ppermute | solution.py:313
  36.6 3.6 %collective-permute-done.7.refs_2_ = f32[8,2,8,128]{3,2,1,0:T(8,128)S(1)} collective-permute-done((f32[8,2,8,128]{3,2,1,0:T(8,128)S(1)}, f32[8,2,8,128]{3,2,1,0:T(8,128)S(1)}, u32[]{:S(2)}, u32[]{:S(2)}) %collective-permute-start.7) | collective-permute-done | bytes 65568 | tf_op jit(solution)/shard_map/ppermute | solution.py:313
  40.7 1.2 %collective-permute-done.14 = f32[8,16,128]{2,1,0:T(8,128)S(1)} collective-permute-done((f32[8,16,128]{2,1,0:T(8,128)S(1)}, f32[8,16,128]{2,1,0:T(8,128)S(1)}, u32[]{:S(2)}, u32[]{:S(2)}) %collective-permute-start.14) | collective-permute-done | bytes 65568 | tf_op jit(solution)/shard_map/ppermute | solution.py:313
  42.0 1.4 %collective-permute-start.15 = (f32[2,8,16,128]{3,2,1,0:T(8,128)S(1)}, f32[2,8,16,128]{3,2,1,0:T(8,128)S(1)}, u32[]{:S(2)}, u32[]{:S(2)}) collective-permute-start(f32[2,8,16,128]{3,2,1,0:T(8,128)S(1)} %pad_maximum_fusion.1.refs_4_), channel_id=1, source_target_pairs={{0,8},{8,0},{16,24},{24,16},{1,9},{9,1},{17,25},{25,17},{2,10},{10... | collective-permute-start | bytes 393224 | tf_op jit(solution)/shard_map/ppermute | solution.py:313
  43.4 1.5 %collective-permute-start.16 = (f32[2,8,16,128]{3,2,1,0:T(8,128)S(1)}, f32[2,8,16,128]{3,2,1,0:T(8,128)S(1)}, u32[]{:S(2)}, u32[]{:S(2)}) collective-permute-start(f32[2,8,16,128]{3,2,1,0:T(8,128)S(1)} %pad_maximum_fusion.1.refs_4_), channel_id=1, source_target_pairs={{0,16},{8,24},{16,0},{24,8},{1,17},{9,25},{17,1},{25,9},{2,18},{10... | collective-permute-start | bytes 393224 | tf_op jit(solution)/shard_map/ppermute | solution.py:313
  44.9 0.6 %collective-permute-start.17 = (f32[2,8,16,128]{3,2,1,0:T(8,128)S(1)}, f32[2,8,16,128]{3,2,1,0:T(8,128)S(1)}, u32[]{:S(2)}, u32[]{:S(2)}) collective-permute-start(f32[2,8,16,128]{3,2,1,0:T(8,128)S(1)} %pad_maximum_fusion.1.refs_4_), channel_id=1, source_target_pairs={{0,24},{8,16},{16,8},{24,0},{1,25},{9,17},{17,9},{25,1},{2,26},{10... | collective-permute-start | bytes 393224 | tf_op jit(solution)/shard_map/ppermute | solution.py:313
  45.6 2.5 %collective-permute-done.15.refs_5_ = f32[2,8,16,128]{3,2,1,0:T(8,128)S(1)} collective-permute-done((f32[2,8,16,128]{3,2,1,0:T(8,128)S(1)}, f32[2,8,16,128]{3,2,1,0:T(8,128)S(1)}, u32[]{:S(2)}, u32[]{:S(2)}) %collective-permute-start.15) | collective-permute-done | bytes 131104 | tf_op jit(solution)/shard_map/ppermute | solution.py:313
  48.1 3.4 %collective-permute-done.16.refs_6_ = f32[2,8,16,128]{3,2,1,0:T(8,128)S(1)} collective-permute-done((f32[2,8,16,128]{3,2,1,0:T(8,128)S(1)}, f32[2,8,16,128]{3,2,1,0:T(8,128)S(1)}, u32[]{:S(2)}, u32[]{:S(2)}) %collective-permute-start.16) | collective-permute-done | bytes 131104 | tf_op jit(solution)/shard_map/ppermute | solution.py:313
  51.5 2.6 %lags.1 = f32[512,128]{1,0:T(8,128)} custom-call(s32[2]{0:T(128)S(1)} %pad_add_fusion.place_ref, s32[3,16]{1,0:T(4,128)S(1)} %copy-done.1, s32[1,128]{1,0:T(1,128)S(1)} %bitcast.32, bf16[320,768]{1,0:T(8,128)(2,1)S(1)} %copy-done, f32[2,8,16,128]{3,2,1,0:T(8,128)S(1)} %pad_maximum_fusion.refs_0_, f32[2,8,16,128]{3,2,1,0:T(8,128)S(1)} %collective-permute-done.8.refs_1_, ...), custom_call_target="tpu_custom_call" | custom-call | tf_op jit(solution)/shard_map/lags/pallas_call | solution.py:301
  (43 shorter events, 2.2 us)
Async XLA Ops:
  0.0 1.8 %copy-start.4 = (f32[64,3,1536]{2,0,1:T(8,128)S(1)}, f32[64,3,1536]{2,0,1:T(8,128)}, u32[]{:S(2)}) copy-start(f32[64,3,1536]{2,0,1:T(8,128)} %param.6) | copy-start | bytes 3538948
  0.0 1.7 %copy-start.5 = (s32[1536]{0:T(1024)S(1)}, s32[1536]{0:T(1024)}, u32[]{:S(2)}) copy-start(s32[1536]{0:T(1024)} %param.7) | copy-start | bytes 18436
  0.0 3.0 %copy-start.1 = (s32[3,16]{1,0:T(4,128)S(1)}, s32[3,16]{1,0:T(4,128)}, u32[]{:S(2)}) copy-start(s32[3,16]{1,0:T(4,128)} %wave_ref.7) | copy-start | bytes 580
  0.0 3.0 %copy-start.3 = (f32[2]{0:T(128)S(1)}, f32[2]{0:T(128)}, u32[]{:S(2)}) copy-start(f32[2]{0:T(128)} %length_ref.5) | copy-start | bytes 28
  1.2 1.8 %collective-permute-start = (f32[48,1536]{1,0:T(8,128)S(1)}, f32[48,1536]{1,0:T(8,128)S(1)}, u32[]{:S(2)}, u32[]{:S(2)}) collective-permute-start(f32[48,1536]{1,0:T(8,128)S(1)} %bitcast.33), channel_id=1, source_target_pairs={{0,1},{1,0},{2,3},{3,2},{4,5},{5,4},{6,7},{7,6},{8,9},{9,8},{10,11... | collective-permute-start | bytes 884744 | tf_op jit(solution)/shard_map/ppermute | solution.py:313
  1.7 1.2 %collective-permute-start.1 = (s32[1536]{0:T(1024)S(1)}, s32[1536]{0:T(1024)S(1)}, u32[]{:S(2)}, u32[]{:S(2)}) collective-permute-start(s32[1536]{0:T(1024)S(1)} %copy-done.5), channel_id=1, source_target_pairs={{0,1},{1,0},{2,3},{3,2},{4,5},{5,4},{6,7},{7,6},{8,9},{9,8},{10,11... | collective-permute-start | bytes 18440 | tf_op jit(solution)/shard_map/ppermute | solution.py:313
  1.9 21.1 %collective-permute-start.5 = (f32[24,1536]{1,0:T(8,128)S(1)}, f32[24,1536]{1,0:T(8,128)S(1)}, u32[]{:S(2)}, u32[]{:S(2)}) collective-permute-start(f32[24,1536]{1,0:T(8,128)S(1)} %get-tuple-element.38), channel_id=1, source_target_pairs={{0,1},{1,0},{2,3},{3,2},{4,5},{5,4},{6,7},{7,6},{8,9},{9,8},{10,11... | collective-permute-start | bytes 442376 | tf_op jit(solution)/shard_map/ppermute | solution.py:313
  2.4 10.9 %collective-permute-start.11 = (f32[24,1536]{1,0:T(8,128)S(1)}, f32[24,1536]{1,0:T(8,128)S(1)}, u32[]{:S(2)}, u32[]{:S(2)}) collective-permute-start(f32[24,1536]{1,0:T(8,128)S(1)} %get-tuple-element.37), channel_id=1, source_target_pairs={{0,1},{1,0},{2,3},{3,2},{4,5},{5,4},{6,7},{7,6},{8,9},{9,8},{10,11... | collective-permute-start | bytes 442376 | tf_op jit(solution)/shard_map/ppermute | solution.py:313
  10.2 9.7 %collective-permute-start.2 = (f32[16,4,8,128]{3,2,1,0:T(8,128)S(1)}, f32[16,4,8,128]{3,2,1,0:T(8,128)S(1)}, u32[]{:S(2)}, u32[]{:S(2)}) collective-permute-start(f32[16,4,8,128]{3,2,1,0:T(8,128)S(1)} %get-tuple-element.22), channel_id=1, source_target_pairs={{0,2},{1,3},{2,0},{3,1},{4,6},{5,7},{6,4},{7,5},{8,10},{9,11},{10,... | collective-permute-start | bytes 786440 | tf_op jit(solution)/shard_map/ppermute | solution.py:313
  17.2 12.3 %collective-permute-start.12 = (f32[8,4,8,128]{3,2,1,0:T(8,128)S(1)}, f32[8,4,8,128]{3,2,1,0:T(8,128)S(1)}, u32[]{:S(2)}, u32[]{:S(2)}) collective-permute-start(f32[8,4,8,128]{3,2,1,0:T(8,128)S(1)} %get-tuple-element.31), channel_id=1, source_target_pairs={{0,2},{1,3},{2,0},{3,1},{4,6},{5,7},{6,4},{7,5},{8,10},{9,11},{10,... | collective-permute-start | bytes 393224 | tf_op jit(solution)/shard_map/ppermute | solution.py:313
  20.0 9.1 %collective-permute-start.3 = (f32[16,2,8,128]{3,2,1,0:T(8,128)S(1)}, f32[16,2,8,128]{3,2,1,0:T(8,128)S(1)}, u32[]{:S(2)}, u32[]{:S(2)}) collective-permute-start(f32[16,2,8,128]{3,2,1,0:T(8,128)S(1)} %slice_add_fusion), channel_id=1, source_target_pairs={{0,4},{1,5},{2,6},{3,7},{4,0},{5,1},{6,2},{7,3},{8,12},{9,13},{10,... | collective-permute-start | bytes 393224 | tf_op jit(solution)/shard_map/ppermute | solution.py:313
  26.9 24.6 %copy-start = (bf16[320,768]{1,0:T(8,128)(2,1)S(1)}, bf16[320,768]{1,0:T(8,128)(2,1)}, u32[]{:S(2)}) copy-start(bf16[320,768]{1,0:T(8,128)(2,1)} %constant.28.clone.basis_ref) | copy-start | bytes 1474564
  26.9 24.6 %copy-start.2 = (s32[128]{0:T(128)S(1)}, s32[128]{0:T(128)}, u32[]{:S(2)}) copy-start(s32[128]{0:T(128)} %param.10) | copy-start | bytes 1540
  26.9 7.4 %collective-permute-start.6 = (f32[8,4,8,128]{3,2,1,0:T(8,128)S(1)}, f32[8,4,8,128]{3,2,1,0:T(8,128)S(1)}, u32[]{:S(2)}, u32[]{:S(2)}) collective-permute-start(f32[8,4,8,128]{3,2,1,0:T(8,128)S(1)} %get-tuple-element.26), channel_id=1, source_target_pairs={{0,2},{1,3},{2,0},{3,1},{4,6},{5,7},{6,4},{7,5},{8,10},{9,11},{10,... | collective-permute-start | bytes 393224 | tf_op jit(solution)/shard_map/ppermute | solution.py:313
  29.4 1.3 %collective-permute-start.4 = (f32[8,16,128]{2,1,0:T(8,128)S(1)}, f32[8,16,128]{2,1,0:T(8,128)S(1)}, u32[]{:S(2)}, u32[]{:S(2)}) collective-permute-start(f32[8,16,128]{2,1,0:T(8,128)S(1)} %get-tuple-element.24), channel_id=1, source_target_pairs={{0,1},{1,0},{2,3},{3,2},{4,5},{5,4},{6,7},{7,6},{8,9},{9,8},{10,11... | collective-permute-start | bytes 196616 | tf_op jit(solution)/shard_map/ppermute | solution.py:313
  29.5 6.9 %collective-permute-start.13 = (f32[8,2,8,128]{3,2,1,0:T(8,128)S(1)}, f32[8,2,8,128]{3,2,1,0:T(8,128)S(1)}, u32[]{:S(2)}, u32[]{:S(2)}) collective-permute-start(f32[8,2,8,128]{3,2,1,0:T(8,128)S(1)} %slice_add_fusion.1), channel_id=1, source_target_pairs={{0,4},{1,5},{2,6},{3,7},{4,0},{5,1},{6,2},{7,3},{8,12},{9,13},{10,... | collective-permute-start | bytes 196616 | tf_op jit(solution)/shard_map/ppermute | solution.py:313
  30.7 9.5 %collective-permute-start.8 = (f32[2,8,16,128]{3,2,1,0:T(8,128)S(1)}, f32[2,8,16,128]{3,2,1,0:T(8,128)S(1)}, u32[]{:S(2)}, u32[]{:S(2)}) collective-permute-start(f32[2,8,16,128]{3,2,1,0:T(8,128)S(1)} %pad_maximum_fusion.refs_0_), channel_id=1, source_target_pairs={{0,8},{8,0},{16,24},{24,16},{1,9},{9,1},{17,25},{25,17},{2,10},{10... | collective-permute-start | bytes 393224 | tf_op jit(solution)/shard_map/ppermute | solution.py:313
  32.3 8.1 %collective-permute-start.9 = (f32[2,8,16,128]{3,2,1,0:T(8,128)S(1)}, f32[2,8,16,128]{3,2,1,0:T(8,128)S(1)}, u32[]{:S(2)}, u32[]{:S(2)}) collective-permute-start(f32[2,8,16,128]{3,2,1,0:T(8,128)S(1)} %pad_maximum_fusion.refs_0_), channel_id=1, source_target_pairs={{0,16},{8,24},{16,0},{24,8},{1,17},{9,25},{17,1},{25,9},{2,18},{10... | collective-permute-start | bytes 393224 | tf_op jit(solution)/shard_map/ppermute | solution.py:313
  33.8 6.6 %collective-permute-start.10 = (f32[2,8,16,128]{3,2,1,0:T(8,128)S(1)}, f32[2,8,16,128]{3,2,1,0:T(8,128)S(1)}, u32[]{:S(2)}, u32[]{:S(2)}) collective-permute-start(f32[2,8,16,128]{3,2,1,0:T(8,128)S(1)} %pad_maximum_fusion.refs_0_), channel_id=1, source_target_pairs={{0,24},{8,16},{16,8},{24,0},{1,25},{9,17},{17,9},{25,1},{2,26},{10... | collective-permute-start | bytes 393224 | tf_op jit(solution)/shard_map/ppermute | solution.py:313
  34.3 5.9 %collective-permute-start.7 = (f32[8,2,8,128]{3,2,1,0:T(8,128)S(1)}, f32[8,2,8,128]{3,2,1,0:T(8,128)S(1)}, u32[]{:S(2)}, u32[]{:S(2)}) collective-permute-start(f32[8,2,8,128]{3,2,1,0:T(8,128)S(1)} %slice_add_fusion.2), channel_id=1, source_target_pairs={{0,4},{1,5},{2,6},{3,7},{4,0},{5,1},{6,2},{7,3},{8,12},{9,13},{10,... | collective-permute-start | bytes 196616 | tf_op jit(solution)/shard_map/ppermute | solution.py:313
  40.6 1.3 %collective-permute-start.14 = (f32[8,16,128]{2,1,0:T(8,128)S(1)}, f32[8,16,128]{2,1,0:T(8,128)S(1)}, u32[]{:S(2)}, u32[]{:S(2)}) collective-permute-start(f32[8,16,128]{2,1,0:T(8,128)S(1)} %pad_maximum_fusion.2), channel_id=1, source_target_pairs={{0,1},{1,0},{2,3},{3,2},{4,5},{5,4},{6,7},{7,6},{8,9},{9,8},{10,11... | collective-permute-start | bytes 196616 | tf_op jit(solution)/shard_map/ppermute | solution.py:313
  42.0 6.1 %collective-permute-start.15 = (f32[2,8,16,128]{3,2,1,0:T(8,128)S(1)}, f32[2,8,16,128]{3,2,1,0:T(8,128)S(1)}, u32[]{:S(2)}, u32[]{:S(2)}) collective-permute-start(f32[2,8,16,128]{3,2,1,0:T(8,128)S(1)} %pad_maximum_fusion.1.refs_4_), channel_id=1, source_target_pairs={{0,8},{8,0},{16,24},{24,16},{1,9},{9,1},{17,25},{25,17},{2,10},{10... | collective-permute-start | bytes 393224 | tf_op jit(solution)/shard_map/ppermute | solution.py:313
  43.4 8.1 %collective-permute-start.16 = (f32[2,8,16,128]{3,2,1,0:T(8,128)S(1)}, f32[2,8,16,128]{3,2,1,0:T(8,128)S(1)}, u32[]{:S(2)}, u32[]{:S(2)}) collective-permute-start(f32[2,8,16,128]{3,2,1,0:T(8,128)S(1)} %pad_maximum_fusion.1.refs_4_), channel_id=1, source_target_pairs={{0,16},{8,24},{16,0},{24,8},{1,17},{9,25},{17,1},{25,9},{2,18},{10... | collective-permute-start | bytes 393224 | tf_op jit(solution)/shard_map/ppermute | solution.py:313
  44.9 6.6 %collective-permute-start.17 = (f32[2,8,16,128]{3,2,1,0:T(8,128)S(1)}, f32[2,8,16,128]{3,2,1,0:T(8,128)S(1)}, u32[]{:S(2)}, u32[]{:S(2)}) collective-permute-start(f32[2,8,16,128]{3,2,1,0:T(8,128)S(1)} %pad_maximum_fusion.1.refs_4_), channel_id=1, source_target_pairs={{0,24},{8,16},{16,8},{24,0},{1,25},{9,17},{17,9},{25,1},{2,26},{10... | collective-permute-start | bytes 393224 | tf_op jit(solution)/shard_map/ppermute | solution.py:313

commit v3 on v2

--- a/solution.py
+++ b/solution.py
@@ -18,6 +18,9 @@
 PITCH = 17
 WIDE = 33
 VMEM_LIMIT = 48 << 20
+WAITS = ()
+BOTH = 0
+WAVES = 1000
 
 
 def polynomial(coefficients, s):
@@ -333,31 +336,37 @@
 
     labels = [species[None, :], swapped(species, "atom", 1)[None, :]]
     place = jnp.stack([tm, me]).astype(jnp.int32)
-    finals, rings = [], []
+    finals, rings, sums = [], [], []
     for c, size in enumerate(sizes):
         start = sum(sizes[:c])
         own = payload(me & 1, start, size)
         sibling = swapped(payload(1 - (me & 1), start, size), "atom", 1)
-        keep, send = density(place[1:2], wave_numbers, lengths, own, sibling, *labels, size // 8, bits, shift)
-        terms, fresh, held = [keep], True, 8
-        for flip in flips:
-            if flip >= (1 << shift):
-                held //= 2
-                out = send if fresh else sum(t[:, held : 2 * held] for t in terms)
-                fresh = False
-                terms = terms + [swapped(out, "atom", flip)]
-            else:
-                keep, send = (a + swapped(a, "atom", flip) for a in (keep, send))
-                terms = [keep]
+        sums.append(list(density(place[1:2], wave_numbers, lengths, own, sibling, *labels, size // 8, bits, shift)))
+    held = [8] * len(sizes)
+    terms = [[keep] for keep, _ in sums]
+    for n, flip in enumerate(flips):
+        for c in range(len(sizes)):
+            if flip < (1 << shift):
+                sums[c] = [a + swapped(a, "atom", flip) for a in sums[c]]
+                terms[c] = sums[c][:1]
+                continue
+            held[c] //= 2
+            out = sums[c][1] if held[c] == 4 else sum(t[:, held[c] : 2 * held[c]] for t in terms[c])
+            terms[c].append(swapped(out, "atom", flip))
+    for c, late, which in WAITS:
+        terms[c][-1], terms[late][which] = lax.optimization_barrier((terms[c][-1], terms[late][which]))
+    for c in range(len(sizes)):
         for chunk, ring in TIES:
             if chunk == c:
-                terms[-1], *rings[ring][1:] = lax.optimization_barrier((terms[-1], *rings[ring][1:]))
-        final = waves(terms, held)
+                terms[c][-1], *rings[ring][3:] = lax.optimization_barrier((terms[c][-1], *rings[ring][3:]))
+        final = waves(terms[c], held[c])
         finals.append((final[0], final[-1]))
         for ring in RINGS:
             if ring[-1] == c:
                 mine, other = (jnp.concatenate([finals[i][j] for i in ring], 1) for j in range(2))
                 both = jnp.stack([mine, swapped(other, "atom", 1)])
+                if c == 0 and BOTH:
+                    both, terms[BOTH][1] = lax.optimization_barrier((both, terms[BOTH][1]))
                 rings.append([both] + [swapped(both, "tm", p) for p in range(1, blocks)])
     parts = [part for ring in rings for part in ring]
     return lags(place, wave_numbers, lag_list, parts, frames * blocks, atoms * devices, period, share)

time: 54.2 us -> 53.1 us (0.980)
  waiting for transfers between devices: 15.1 us -> 11.5 us
  starting transfers between devices: 19 us -> 21.4 us
    ppermute x18, waiting for transfers between devices: 15.1 us -> 11.5 us  [swapped(): lax.ppermute(block, axis, [(i, i ^ flip) for i in range(lax.axis_size(axi...]
    ppermute x18, starting transfers between devices: 19 us -> 21.4 us  [swapped(): lax.ppermute(block, axis, [(i, i ^ flip) for i in range(lax.axis_size(axi...]
  transfers between devices with their start and end apart: 18 -> 18, of which waited for: 9 -> 7; matrix products, arithmetic and copies ran while one was open for 0% -> 0% of each run, Pallas kernels for 29% -> 30%
where the time goes in v3:
time: 53.1 us; the launch traced here: 52.9 us
  starting transfers between devices  21.4 us (40%)
  Pallas kernels  18.4 us (35%)
  waiting for transfers between devices  11.5 us (22%)
  local copies, waits for them, and re-layouts  1.28 us (2%)
    ppermute x18, starting transfers between devices, swapped(): lax.ppermute(block, axis, [(i, i ^ flip) for i in range(lax.axis_size(axi...  21.4 us
    pallas_call x3, Pallas kernels, density(): pl.pallas_call(functools.partial(density_kernel, groups=groups, bits=bits...  15 us
    ppermute x18, waiting for transfers between devices, swapped(): lax.ppermute(block, axis, [(i, i ^ flip) for i in range(lax.axis_size(axi...  11.5 us
    pallas_call x1, Pallas kernels, lags(): pl.pallas_call(functools.partial(lags_kernel, blocks=len(parts), frames=f...  2.56 us
    another operation x1, local copies, waits for them, and re-layouts  1.2 us
  transfers between devices with their start and end apart: 18, of which 7 were waited for; matrix products, arithmetic and copies ran while one was open for 0% of the time, Pallas kernels for 30%

profile of v3, /device:TPU:0, one launch (start us, length us, event | category | flops | bytes accessed | tf_op | source)
XLA Modules:
  0.0 52.9 jit_solution(11475809419006171423)
XLA Ops:
  0.0 1.2 %constant_dynamic-slice_fusion = (f32[16,3,1536]{2,0,1:T(8,128)S(1)}, f32[16,3,1536]{2,0,1:T(8,128)S(1)}) fusion(f32[64,3,1536]{2,0,1:T(8,128)} %param.6, s32[]{:T(128)S(6)} %select_n.19, s32[]{:T(128)S(6)} %select_n.18), kind=kLoop, calls=%fused_computation.11 | loop fusion | bytes 1179656 | tf_op jit(solution)/shard_map/dynamic-slice.1
  1.2 0.5 collective-permute-start
  1.9 0.5 collective-permute-start.7
  2.5 0.5 collective-permute-done.1
  3.0 7.2 %density.3 = (f32[16,4,8,128]{3,2,1,0:T(8,128)S(1)}, f32[16,4,8,128]{3,2,1,0:T(8,128)S(1)}) custom-call(s32[1]{0:T(128)} %bitcast.1.me_ref, s32[3,16]{1,0:T(4,128)S(1)} %copy-done.1, f32[2]{0:T(128)S(1)} %copy-done.3, f32[48,1536]{1,0:T(8,128)S(1)} %bitcast.30, f32[48,1536]{1,0:T(8,128)S(1)} %collective-permute-done.sibling_ref, ...), custom_call_target="tpu_custom_call" | custom-call | flops 6442450944 | bytes 524288 | tf_op jit(solution)/shard_map/density/pallas_call | solution.py:170
  10.2 3.0 %collective-permute-start.2 = (f32[16,4,8,128]{3,2,1,0:T(8,128)S(1)}, f32[16,4,8,128]{3,2,1,0:T(8,128)S(1)}, u32[]{:S(2)}, u32[]{:S(2)}) collective-permute-start(f32[16,4,8,128]{3,2,1,0:T(8,128)S(1)} %get-tuple-element.20), channel_id=1, source_target_pairs={{0,2},{1,3},{2,0},{3,1},{4,6},{5,7},{6,4},{7,5},{8,10},{9,11},{10,... | collective-permute-start | bytes 786440 | tf_op jit(solution)/shard_map/ppermute | solution.py:316
  13.2 3.9 %density.5 = (f32[8,4,8,128]{3,2,1,0:T(8,128)S(1)}, f32[8,4,8,128]{3,2,1,0:T(8,128)S(1)}) custom-call(s32[1]{0:T(128)} %bitcast.1.me_ref, s32[3,16]{1,0:T(4,128)S(1)} %copy-done.1, f32[2]{0:T(128)S(1)} %copy-done.3, f32[24,1536]{1,0:T(8,128)S(1)} %get-tuple-element.36.own_ref, f32[24,1536]{1,0:T(8,128)S(1)} %collective-permute-done.11.sibling_ref, ...), custom_call_target="tpu_custom_call" | custom-call | flops 3221225472 | bytes 262144 | tf_op jit(solution)/shard_map/density/pallas_call | solution.py:170
  17.2 2.7 %collective-permute-done.2.refs_1_ = f32[16,4,8,128]{3,2,1,0:T(8,128)S(1)} collective-permute-done((f32[16,4,8,128]{3,2,1,0:T(8,128)S(1)}, f32[16,4,8,128]{3,2,1,0:T(8,128)S(1)}, u32[]{:S(2)}, u32[]{:S(2)}) %collective-permute-start.2) | collective-permute-done | bytes 262176 | tf_op jit(solution)/shard_map/ppermute | solution.py:316
  20.0 3.0 %collective-permute-start.3 = (f32[16,2,8,128]{3,2,1,0:T(8,128)S(1)}, f32[16,2,8,128]{3,2,1,0:T(8,128)S(1)}, u32[]{:S(2)}, u32[]{:S(2)}) collective-permute-start(f32[16,2,8,128]{3,2,1,0:T(8,128)S(1)} %slice_add_fusion), channel_id=1, source_target_pairs={{0,4},{1,5},{2,6},{3,7},{4,0},{5,1},{6,2},{7,3},{8,12},{9,13},{10,... | collective-permute-start | bytes 393224 | tf_op jit(solution)/shard_map/ppermute | solution.py:316
  23.0 3.9 %density.4 = (f32[8,4,8,128]{3,2,1,0:T(8,128)S(1)}, f32[8,4,8,128]{3,2,1,0:T(8,128)S(1)}) custom-call(s32[1]{0:T(128)} %bitcast.1.me_ref, s32[3,16]{1,0:T(4,128)S(1)} %copy-done.1, f32[2]{0:T(128)S(1)} %copy-done.3, f32[24,1536]{1,0:T(8,128)S(1)} %get-tuple-element.35.own_ref, f32[24,1536]{1,0:T(8,128)S(1)} %collective-permute-done.7.sibling_ref, ...), custom_call_target="tpu_custom_call" | custom-call | flops 3221225472 | bytes 262144 | tf_op jit(solution)/shard_map/density/pallas_call | solution.py:170
  26.9 2.2 %collective-permute-start.8 = (f32[8,4,8,128]{3,2,1,0:T(8,128)S(1)}, f32[8,4,8,128]{3,2,1,0:T(8,128)S(1)}, u32[]{:S(2)}, u32[]{:S(2)}) collective-permute-start(f32[8,4,8,128]{3,2,1,0:T(8,128)S(1)} %get-tuple-element.24), channel_id=1, source_target_pairs={{0,2},{1,3},{2,0},{3,1},{4,6},{5,7},{6,4},{7,5},{8,10},{9,11},{10,... | collective-permute-start | bytes 393224 | tf_op jit(solution)/shard_map/ppermute | solution.py:316
  29.9 0.8 %collective-permute-done.4 = f32[8,16,128]{2,1,0:T(8,128)S(1)} collective-permute-done((f32[8,16,128]{2,1,0:T(8,128)S(1)}, f32[8,16,128]{2,1,0:T(8,128)S(1)}, u32[]{:S(2)}, u32[]{:S(2)}) %collective-permute-start.4) | collective-permute-done | bytes 65568 | tf_op jit(solution)/shard_map/ppermute | solution.py:316
  30.7 2.5 %collective-permute-start.10 = (f32[2,8,16,128]{3,2,1,0:T(8,128)S(1)}, f32[2,8,16,128]{3,2,1,0:T(8,128)S(1)}, u32[]{:S(2)}, u32[]{:S(2)}) collective-permute-start(f32[2,8,16,128]{3,2,1,0:T(8,128)S(1)} %pad_maximum_fusion.refs_0_), channel_id=1, source_target_pairs={{0,24},{8,16},{16,8},{24,0},{1,25},{9,17},{17,9},{25,1},{2,26},{10... | collective-permute-start | bytes 393224 | tf_op jit(solution)/shard_map/ppermute | solution.py:316
  33.2 1.8 %collective-permute-start.9 = (f32[8,2,8,128]{3,2,1,0:T(8,128)S(1)}, f32[8,2,8,128]{3,2,1,0:T(8,128)S(1)}, u32[]{:S(2)}, u32[]{:S(2)}) collective-permute-start(f32[8,2,8,128]{3,2,1,0:T(8,128)S(1)} %slice_add_fusion.2), channel_id=1, source_target_pairs={{0,4},{1,5},{2,6},{3,7},{4,0},{5,1},{6,2},{7,3},{8,12},{9,13},{10,... | collective-permute-start | bytes 196616 | tf_op jit(solution)/shard_map/ppermute | solution.py:316
  35.1 1.2 %collective-permute-done.13.refs_2_ = f32[8,2,8,128]{3,2,1,0:T(8,128)S(1)} collective-permute-done((f32[8,2,8,128]{3,2,1,0:T(8,128)S(1)}, f32[8,2,8,128]{3,2,1,0:T(8,128)S(1)}, u32[]{:S(2)}, u32[]{:S(2)}) %collective-permute-start.13) | collective-permute-done | bytes 65568 | tf_op jit(solution)/shard_map/ppermute | solution.py:316
  36.6 2.0 %collective-permute-start.5 = (f32[2,8,16,128]{3,2,1,0:T(8,128)S(1)}, f32[2,8,16,128]{3,2,1,0:T(8,128)S(1)}, u32[]{:S(2)}, u32[]{:S(2)}) collective-permute-start(f32[2,8,16,128]{3,2,1,0:T(8,128)S(1)} %pad_maximum_fusion.refs_0_), channel_id=1, source_target_pairs={{0,8},{8,0},{16,24},{24,16},{1,9},{9,1},{17,25},{25,17},{2,10},{10... | collective-permute-start | bytes 393224 | tf_op jit(solution)/shard_map/ppermute | solution.py:316
  38.6 1.5 %collective-permute-start.6 = (f32[2,8,16,128]{3,2,1,0:T(8,128)S(1)}, f32[2,8,16,128]{3,2,1,0:T(8,128)S(1)}, u32[]{:S(2)}, u32[]{:S(2)}) collective-permute-start(f32[2,8,16,128]{3,2,1,0:T(8,128)S(1)} %pad_maximum_fusion.refs_0_), channel_id=1, source_target_pairs={{0,16},{8,24},{16,0},{24,8},{1,17},{9,25},{17,1},{25,9},{2,18},{10... | collective-permute-start | bytes 393224 | tf_op jit(solution)/shard_map/ppermute | solution.py:316
  40.5 1.2 %collective-permute-done.14 = f32[8,16,128]{2,1,0:T(8,128)S(1)} collective-permute-done((f32[8,16,128]{2,1,0:T(8,128)S(1)}, f32[8,16,128]{2,1,0:T(8,128)S(1)}, u32[]{:S(2)}, u32[]{:S(2)}) %collective-permute-start.14) | collective-permute-done | bytes 65568 | tf_op jit(solution)/shard_map/ppermute | solution.py:316
  41.7 0.6 %collective-permute-start.15 = (f32[2,8,16,128]{3,2,1,0:T(8,128)S(1)}, f32[2,8,16,128]{3,2,1,0:T(8,128)S(1)}, u32[]{:S(2)}, u32[]{:S(2)}) collective-permute-start(f32[2,8,16,128]{3,2,1,0:T(8,128)S(1)} %pad_maximum_fusion.1.refs_4_), channel_id=1, source_target_pairs={{0,8},{8,0},{16,24},{24,16},{1,9},{9,1},{17,25},{25,17},{2,10},{10... | collective-permute-start | bytes 393224 | tf_op jit(solution)/shard_map/ppermute | solution.py:316
  42.3 0.9 %collective-permute-start.16 = (f32[2,8,16,128]{3,2,1,0:T(8,128)S(1)}, f32[2,8,16,128]{3,2,1,0:T(8,128)S(1)}, u32[]{:S(2)}, u32[]{:S(2)}) collective-permute-start(f32[2,8,16,128]{3,2,1,0:T(8,128)S(1)} %pad_maximum_fusion.1.refs_4_), channel_id=1, source_target_pairs={{0,16},{8,24},{16,0},{24,8},{1,17},{9,25},{17,1},{25,9},{2,18},{10... | collective-permute-start | bytes 393224 | tf_op jit(solution)/shard_map/ppermute | solution.py:316
  43.1 2.1 %collective-permute-start.17 = (f32[2,8,16,128]{3,2,1,0:T(8,128)S(1)}, f32[2,8,16,128]{3,2,1,0:T(8,128)S(1)}, u32[]{:S(2)}, u32[]{:S(2)}) collective-permute-start(f32[2,8,16,128]{3,2,1,0:T(8,128)S(1)} %pad_maximum_fusion.1.refs_4_), channel_id=1, source_target_pairs={{0,24},{8,16},{16,8},{24,0},{1,25},{9,17},{17,9},{25,1},{2,26},{10... | collective-permute-start | bytes 393224 | tf_op jit(solution)/shard_map/ppermute | solution.py:316
  45.3 2.8 %collective-permute-done.15.refs_5_ = f32[2,8,16,128]{3,2,1,0:T(8,128)S(1)} collective-permute-done((f32[2,8,16,128]{3,2,1,0:T(8,128)S(1)}, f32[2,8,16,128]{3,2,1,0:T(8,128)S(1)}, u32[]{:S(2)}, u32[]{:S(2)}) %collective-permute-start.15) | collective-permute-done | bytes 131104 | tf_op jit(solution)/shard_map/ppermute | solution.py:316
  48.1 2.3 %collective-permute-done.16.refs_6_ = f32[2,8,16,128]{3,2,1,0:T(8,128)S(1)} collective-permute-done((f32[2,8,16,128]{3,2,1,0:T(8,128)S(1)}, f32[2,8,16,128]{3,2,1,0:T(8,128)S(1)}, u32[]{:S(2)}, u32[]{:S(2)}) %collective-permute-start.16) | collective-permute-done | bytes 131104 | tf_op jit(solution)/shard_map/ppermute | solution.py:316
  50.4 2.6 %lags.1 = f32[512,128]{1,0:T(8,128)} custom-call(s32[2]{0:T(128)S(1)} %pad_add_fusion.place_ref, s32[3,16]{1,0:T(4,128)S(1)} %copy-done.1, s32[1,128]{1,0:T(1,128)S(1)} %bitcast.32, bf16[320,768]{1,0:T(8,128)(2,1)S(1)} %copy-done, f32[2,8,16,128]{3,2,1,0:T(8,128)S(1)} %pad_maximum_fusion.refs_0_, f32[2,8,16,128]{3,2,1,0:T(8,128)S(1)} %collective-permute-done.5.refs_1_, ...), custom_call_target="tpu_custom_call" | custom-call | tf_op jit(solution)/shard_map/lags/pallas_call | solution.py:304
  (43 shorter events, 1.9 us)
Async XLA Ops:
  0.0 1.8 %copy-start.4 = (f32[64,3,1536]{2,0,1:T(8,128)S(1)}, f32[64,3,1536]{2,0,1:T(8,128)}, u32[]{:S(2)}) copy-start(f32[64,3,1536]{2,0,1:T(8,128)} %param.6) | copy-start | bytes 3538948
  0.0 1.7 %copy-start.5 = (s32[1536]{0:T(1024)S(1)}, s32[1536]{0:T(1024)}, u32[]{:S(2)}) copy-start(s32[1536]{0:T(1024)} %param.7) | copy-start | bytes 18436
  0.0 3.0 %copy-start.1 = (s32[3,16]{1,0:T(4,128)S(1)}, s32[3,16]{1,0:T(4,128)}, u32[]{:S(2)}) copy-start(s32[3,16]{1,0:T(4,128)} %wave_ref.7) | copy-start | bytes 580
  0.0 3.0 %copy-start.3 = (f32[2]{0:T(128)S(1)}, f32[2]{0:T(128)}, u32[]{:S(2)}) copy-start(f32[2]{0:T(128)} %length_ref.5) | copy-start | bytes 28
  1.2 1.8 %collective-permute-start = (f32[48,1536]{1,0:T(8,128)S(1)}, f32[48,1536]{1,0:T(8,128)S(1)}, u32[]{:S(2)}, u32[]{:S(2)}) collective-permute-start(f32[48,1536]{1,0:T(8,128)S(1)} %bitcast.33), channel_id=1, source_target_pairs={{0,1},{1,0},{2,3},{3,2},{4,5},{5,4},{6,7},{7,6},{8,9},{9,8},{10,11... | collective-permute-start | bytes 884744 | tf_op jit(solution)/shard_map/ppermute | solution.py:316
  1.7 1.2 %collective-permute-start.1 = (s32[1536]{0:T(1024)S(1)}, s32[1536]{0:T(1024)S(1)}, u32[]{:S(2)}, u32[]{:S(2)}) collective-permute-start(s32[1536]{0:T(1024)S(1)} %copy-done.5), channel_id=1, source_target_pairs={{0,1},{1,0},{2,3},{3,2},{4,5},{5,4},{6,7},{7,6},{8,9},{9,8},{10,11... | collective-permute-start | bytes 18440 | tf_op jit(solution)/shard_map/ppermute | solution.py:316
  1.9 21.1 %collective-permute-start.7 = (f32[24,1536]{1,0:T(8,128)S(1)}, f32[24,1536]{1,0:T(8,128)S(1)}, u32[]{:S(2)}, u32[]{:S(2)}) collective-permute-start(f32[24,1536]{1,0:T(8,128)S(1)} %get-tuple-element.34), channel_id=1, source_target_pairs={{0,1},{1,0},{2,3},{3,2},{4,5},{5,4},{6,7},{7,6},{8,9},{9,8},{10,11... | collective-permute-start | bytes 442376 | tf_op jit(solution)/shard_map/ppermute | solution.py:316
  2.4 10.9 %collective-permute-start.11 = (f32[24,1536]{1,0:T(8,128)S(1)}, f32[24,1536]{1,0:T(8,128)S(1)}, u32[]{:S(2)}, u32[]{:S(2)}) collective-permute-start(f32[24,1536]{1,0:T(8,128)S(1)} %get-tuple-element.33), channel_id=1, source_target_pairs={{0,1},{1,0},{2,3},{3,2},{4,5},{5,4},{6,7},{7,6},{8,9},{9,8},{10,11... | collective-permute-start | bytes 442376 | tf_op jit(solution)/shard_map/ppermute | solution.py:316
  10.2 9.7 %collective-permute-start.2 = (f32[16,4,8,128]{3,2,1,0:T(8,128)S(1)}, f32[16,4,8,128]{3,2,1,0:T(8,128)S(1)}, u32[]{:S(2)}, u32[]{:S(2)}) collective-permute-start(f32[16,4,8,128]{3,2,1,0:T(8,128)S(1)} %get-tuple-element.20), channel_id=1, source_target_pairs={{0,2},{1,3},{2,0},{3,1},{4,6},{5,7},{6,4},{7,5},{8,10},{9,11},{10,... | collective-permute-start | bytes 786440 | tf_op jit(solution)/shard_map/ppermute | solution.py:316
  17.2 12.3 %collective-permute-start.12 = (f32[8,4,8,128]{3,2,1,0:T(8,128)S(1)}, f32[8,4,8,128]{3,2,1,0:T(8,128)S(1)}, u32[]{:S(2)}, u32[]{:S(2)}) collective-permute-start(f32[8,4,8,128]{3,2,1,0:T(8,128)S(1)} %get-tuple-element.27), channel_id=1, source_target_pairs={{0,2},{1,3},{2,0},{3,1},{4,6},{5,7},{6,4},{7,5},{8,10},{9,11},{10,... | collective-permute-start | bytes 393224 | tf_op jit(solution)/shard_map/ppermute | solution.py:316
  20.0 9.1 %collective-permute-start.3 = (f32[16,2,8,128]{3,2,1,0:T(8,128)S(1)}, f32[16,2,8,128]{3,2,1,0:T(8,128)S(1)}, u32[]{:S(2)}, u32[]{:S(2)}) collective-permute-start(f32[16,2,8,128]{3,2,1,0:T(8,128)S(1)} %slice_add_fusion), channel_id=1, source_target_pairs={{0,4},{1,5},{2,6},{3,7},{4,0},{5,1},{6,2},{7,3},{8,12},{9,13},{10,... | collective-permute-start | bytes 393224 | tf_op jit(solution)/shard_map/ppermute | solution.py:316
  26.9 23.5 %copy-start = (bf16[320,768]{1,0:T(8,128)(2,1)S(1)}, bf16[320,768]{1,0:T(8,128)(2,1)}, u32[]{:S(2)}) copy-start(bf16[320,768]{1,0:T(8,128)(2,1)} %constant.28.clone.basis_ref) | copy-start | bytes 1474564
  26.9 23.5 %copy-start.2 = (s32[128]{0:T(128)S(1)}, s32[128]{0:T(128)}, u32[]{:S(2)}) copy-start(s32[128]{0:T(128)} %param.10) | copy-start | bytes 1540
  26.9 6.3 %collective-permute-start.8 = (f32[8,4,8,128]{3,2,1,0:T(8,128)S(1)}, f32[8,4,8,128]{3,2,1,0:T(8,128)S(1)}, u32[]{:S(2)}, u32[]{:S(2)}) collective-permute-start(f32[8,4,8,128]{3,2,1,0:T(8,128)S(1)} %get-tuple-element.24), channel_id=1, source_target_pairs={{0,2},{1,3},{2,0},{3,1},{4,6},{5,7},{6,4},{7,5},{8,10},{9,11},{10,... | collective-permute-start | bytes 393224 | tf_op jit(solution)/shard_map/ppermute | solution.py:316
  29.4 1.3 %collective-permute-start.4 = (f32[8,16,128]{2,1,0:T(8,128)S(1)}, f32[8,16,128]{2,1,0:T(8,128)S(1)}, u32[]{:S(2)}, u32[]{:S(2)}) collective-permute-start(f32[8,16,128]{2,1,0:T(8,128)S(1)} %get-tuple-element.22), channel_id=1, source_target_pairs={{0,1},{1,0},{2,3},{3,2},{4,5},{5,4},{6,7},{7,6},{8,9},{9,8},{10,11... | collective-permute-start | bytes 196616 | tf_op jit(solution)/shard_map/ppermute | solution.py:316
  29.5 6.9 %collective-permute-start.13 = (f32[8,2,8,128]{3,2,1,0:T(8,128)S(1)}, f32[8,2,8,128]{3,2,1,0:T(8,128)S(1)}, u32[]{:S(2)}, u32[]{:S(2)}) collective-permute-start(f32[8,2,8,128]{3,2,1,0:T(8,128)S(1)} %slice_add_fusion.1), channel_id=1, source_target_pairs={{0,4},{1,5},{2,6},{3,7},{4,0},{5,1},{6,2},{7,3},{8,12},{9,13},{10,... | collective-permute-start | bytes 196616 | tf_op jit(solution)/shard_map/ppermute | solution.py:316
  30.7 9.4 %collective-permute-start.10 = (f32[2,8,16,128]{3,2,1,0:T(8,128)S(1)}, f32[2,8,16,128]{3,2,1,0:T(8,128)S(1)}, u32[]{:S(2)}, u32[]{:S(2)}) collective-permute-start(f32[2,8,16,128]{3,2,1,0:T(8,128)S(1)} %pad_maximum_fusion.refs_0_), channel_id=1, source_target_pairs={{0,24},{8,16},{16,8},{24,0},{1,25},{9,17},{17,9},{25,1},{2,26},{10... | collective-permute-start | bytes 393224 | tf_op jit(solution)/shard_map/ppermute | solution.py:316
  33.2 6.8 %collective-permute-start.9 = (f32[8,2,8,128]{3,2,1,0:T(8,128)S(1)}, f32[8,2,8,128]{3,2,1,0:T(8,128)S(1)}, u32[]{:S(2)}, u32[]{:S(2)}) collective-permute-start(f32[8,2,8,128]{3,2,1,0:T(8,128)S(1)} %slice_add_fusion.2), channel_id=1, source_target_pairs={{0,4},{1,5},{2,6},{3,7},{4,0},{5,1},{6,2},{7,3},{8,12},{9,13},{10,... | collective-permute-start | bytes 196616 | tf_op jit(solution)/shard_map/ppermute | solution.py:316
  36.6 8.7 %collective-permute-start.5 = (f32[2,8,16,128]{3,2,1,0:T(8,128)S(1)}, f32[2,8,16,128]{3,2,1,0:T(8,128)S(1)}, u32[]{:S(2)}, u32[]{:S(2)}) collective-permute-start(f32[2,8,16,128]{3,2,1,0:T(8,128)S(1)} %pad_maximum_fusion.refs_0_), channel_id=1, source_target_pairs={{0,8},{8,0},{16,24},{24,16},{1,9},{9,1},{17,25},{25,17},{2,10},{10... | collective-permute-start | bytes 393224 | tf_op jit(solution)/shard_map/ppermute | solution.py:316
  38.6 6.8 %collective-permute-start.6 = (f32[2,8,16,128]{3,2,1,0:T(8,128)S(1)}, f32[2,8,16,128]{3,2,1,0:T(8,128)S(1)}, u32[]{:S(2)}, u32[]{:S(2)}) collective-permute-start(f32[2,8,16,128]{3,2,1,0:T(8,128)S(1)} %pad_maximum_fusion.refs_0_), channel_id=1, source_target_pairs={{0,16},{8,24},{16,0},{24,8},{1,17},{9,25},{17,1},{25,9},{2,18},{10... | collective-permute-start | bytes 393224 | tf_op jit(solution)/shard_map/ppermute | solution.py:316
  40.4 1.3 %collective-permute-start.14 = (f32[8,16,128]{2,1,0:T(8,128)S(1)}, f32[8,16,128]{2,1,0:T(8,128)S(1)}, u32[]{:S(2)}, u32[]{:S(2)}) collective-permute-start(f32[8,16,128]{2,1,0:T(8,128)S(1)} %pad_maximum_fusion.2), channel_id=1, source_target_pairs={{0,1},{1,0},{2,3},{3,2},{4,5},{5,4},{6,7},{7,6},{8,9},{9,8},{10,11... | collective-permute-start | bytes 196616 | tf_op jit(solution)/shard_map/ppermute | solution.py:316
  41.7 6.4 %collective-permute-start.15 = (f32[2,8,16,128]{3,2,1,0:T(8,128)S(1)}, f32[2,8,16,128]{3,2,1,0:T(8,128)S(1)}, u32[]{:S(2)}, u32[]{:S(2)}) collective-permute-start(f32[2,8,16,128]{3,2,1,0:T(8,128)S(1)} %pad_maximum_fusion.1.refs_4_), channel_id=1, source_target_pairs={{0,8},{8,0},{16,24},{24,16},{1,9},{9,1},{17,25},{25,17},{2,10},{10... | collective-permute-start | bytes 393224 | tf_op jit(solution)/shard_map/ppermute | solution.py:316
  42.3 8.1 %collective-permute-start.16 = (f32[2,8,16,128]{3,2,1,0:T(8,128)S(1)}, f32[2,8,16,128]{3,2,1,0:T(8,128)S(1)}, u32[]{:S(2)}, u32[]{:S(2)}) collective-permute-start(f32[2,8,16,128]{3,2,1,0:T(8,128)S(1)} %pad_maximum_fusion.1.refs_4_), channel_id=1, source_target_pairs={{0,16},{8,24},{16,0},{24,8},{1,17},{9,25},{17,1},{25,9},{2,18},{10... | collective-permute-start | bytes 393224 | tf_op jit(solution)/shard_map/ppermute | solution.py:316
  43.1 7.2 %collective-permute-start.17 = (f32[2,8,16,128]{3,2,1,0:T(8,128)S(1)}, f32[2,8,16,128]{3,2,1,0:T(8,128)S(1)}, u32[]{:S(2)}, u32[]{:S(2)}) collective-permute-start(f32[2,8,16,128]{3,2,1,0:T(8,128)S(1)} %pad_maximum_fusion.1.refs_4_), channel_id=1, source_target_pairs={{0,24},{8,16},{16,8},{24,0},{1,25},{9,17},{17,9},{25,1},{2,26},{10... | collective-permute-start | bytes 393224 | tf_op jit(solution)/shard_map/ppermute | solution.py:316
